TPU v7x, 32 devices: a whole 2x2x4 slice. The times are simulated.
32 devices in a mesh: ctx: 8 (over z, y), head: 4 (over x, core).
Axes of the slice: x: 2, y: 2, z: 4, core: 2. Of those that a mesh axis runs over, the one named last changes fastest.
Arguments:
- tokens: bfloat16 [2048, 1024], P('ctx', 'head')
- gain: float32 [1024], replicated, may hold values from 0.25 to 1.75
- w_query: bfloat16 [1024, 1024], P(None, 'head'), may hold values from -0.1875 to 0.1875
- w_key: bfloat16 [1024, 1024], P(None, 'head'), may hold values from -0.1875 to 0.1875
- w_value: bfloat16 [1024, 1024], P(None, 'head'), may hold values from -0.1875 to 0.1875
- w_out: bfloat16 [1024, 1024], P('head'), may hold values from -0.1875 to 0.1875
- temper: float32 [16], P('head'), may hold values from 4 to 12
- adjacency: int32 [16, 16], replicated, may hold values from 0 to 1, as said below
- order: int32 [16], replicated, may hold values from 0 to 15, each once
Outputs:
- update: bfloat16 [2048, 1024], P('ctx', 'head')
Inputs may be any that keep to these rules, and one draw needn't show every extreme that they name: Entries are 0 or 1; adjacency[a][a] is 1 for every compartment block a. `order`: each compartment block appears once.
All inputs are finite; a program needn't handle non-finite values.
Results may differ from a plain program's by a relative error of at most 0.015.
Values may be sent and summed in bfloat16 or wider, within the bound.
A program may use at most 64 MiB of HBM per device.

v0:
```python
import jax
import jax.numpy as jnp
from jax import lax
from jax.sharding import PartitionSpec as P

BLOCK = 128


def shifted(shard, axis, by):
    length = lax.axis_size(axis)
    return lax.ppermute(shard, axis, [(i, (i + by) % length) for i in range(length)])


def normalize(values):
    return values * lax.rsqrt(jnp.mean(values * values, axis=-1, keepdims=True) + 1e-06)


def shards(tokens, gain, w_query, w_key, w_value, w_out, temper, adjacency, order):
    whole = lax.all_gather(tokens, "head", axis=1, tiled=True)
    normed = (normalize(whole.astype(jnp.float32)) * gain).astype(jnp.bfloat16)
    rows = whole.shape[0]
    heads = temper.shape[0]
    width = w_query.shape[1]
    size = width // heads
    query = normalize(
        jnp.dot(normed, w_query, preferred_element_type=jnp.float32).reshape(rows, heads, size)
    )
    query = (query * (temper[None, :, None] / size)).astype(jnp.bfloat16)
    keys = normalize(
        jnp.dot(normed, w_key, preferred_element_type=jnp.float32).reshape(rows, heads, size)
    )
    keys = keys.astype(jnp.bfloat16).reshape(rows, width)
    values = jnp.dot(normed, w_value, preferred_element_type=jnp.float32).astype(jnp.bfloat16)
    stacked = jnp.stack([keys, values])
    cycle = lax.axis_size("ctx")
    place = lax.axis_index("ctx")
    local_blocks = rows // BLOCK
    linked = adjacency[order][:, order]
    mine = lax.dynamic_slice_in_dim(linked, place * local_blocks, local_blocks, 0)
    query_live = jnp.repeat(mine, BLOCK, axis=0)

    def attend(carry, piece, start):
        count = piece.shape[1]
        key_block = (start + jnp.arange(count, dtype=jnp.int32)) // BLOCK
        allowed = (jnp.take(query_live, key_block, axis=1) > 0) & True

        def compute(state):
            summed, weight = state
            keys_piece = piece[0].reshape(count, heads, size)
            values_piece = piece[1].reshape(count, heads, size)
            scores = jnp.einsum(
                "qhd,khd->hqk", query, keys_piece, preferred_element_type=jnp.float32
            )
            probs = jnp.where(allowed[None], jnp.exp(scores), 0.0)
            weight = weight + jnp.sum(probs, axis=-1)
            summed = summed + jnp.einsum(
                "hqk,khd->qhd",
                probs.astype(jnp.bfloat16),
                values_piece,
                preferred_element_type=jnp.float32,
            )
            return (summed, weight)

        def keep(state):
            return state

        return lax.cond(jnp.any(allowed), compute, keep, carry)

    initial = (jnp.zeros((rows, heads, size), jnp.float32), jnp.zeros((heads, rows), jnp.float32))
    state = attend(initial, stacked, place * rows)

    def turn(step, pack):
        moving, state = pack
        moving = shifted(moving, "ctx", 1)
        source = (place - step - 1) % cycle
        return (moving, attend(state, moving, source * rows))

    moved, state = lax.fori_loop(0, cycle - 1, turn, (stacked, state))
    summed, weight = state
    attended = (summed / weight.T[:, :, None]).astype(jnp.bfloat16).reshape(rows, width)
    partial_value = jnp.dot(attended, w_out, preferred_element_type=jnp.float32)
    return lax.psum_scatter(
        partial_value.astype(jnp.bfloat16), "head", scatter_dimension=1, tiled=True
    )


def solution(mesh):
    in_specs = (
        P("ctx", "head"),
        P(),
        P(None, "head"),
        P(None, "head"),
        P(None, "head"),
        P("head", None),
        P("head"),
        P(),
        P(),
    )
    out_specs = P("ctx", "head")
    return jax.shard_map(shards, mesh=mesh, in_specs=in_specs, out_specs=out_specs, check_vma=False)
```

profile of v0, /device:TPU:0, one launch (start us, length us, event | category | flops | bytes accessed | tf_op | source)
XLA Modules:
  0.0 121.3 jit_solution(6226943880378041395)
XLA Ops:
  6.6 0.7 copy-done.7
  7.4 0.6 gather_fusion.1
  7.9 0.1 copy.13
  8.0 0.6 gather_fusion.2
  8.6 0.1 dynamic-slice_bitcast_fusion
  8.6 0.1 broadcast_in_dim.51
  8.7 1.0 gather_fusion.3
  9.7 0.8 fusion.17
  11.1 8.8 %all_gather.3 = bf16[256,1024]{1,0:T(8,128)(2,1)S(1)} all-gather(bf16[256,256]{1,0:T(8,128)(2,1)S(1)} %copy-done.2), channel_id=1, replica_groups=mesh['ctx'=8,'head'=4] {'head'}, dimensions={1}, use_global_device_ids=true | all-gather | bytes 655360 | tf_op jit(solution)/shard_map/all_gather | solution.py:19
  19.9 0.2 fusion.7
  20.1 0.5 copy-done.6
  20.6 0.5 convolution_convert_fusion.1
  21.0 0.6 copy-done.4
  21.6 0.5 multiply_reduce_fusion
  22.1 0.6 copy-done.5
  22.6 0.5 multiply_reduce_fusion.1
  23.2 0.1 multiply_convert_fusion
  23.3 0.6 conditional.2
  23.3 0.4 fusion.18
  23.8 0.2 convolution_bitcast_fusion
  24.0 70.7 %while.21 = (s32[]{:T(128)}, bf16[2,256,256]{1,2,0:T(8,128)(2,1)S(1)}, f32[256,4,64]{0,2,1:T(8,128)S(1)}, f32[4,256]{1,0:T(4,128)S(1)}, s32[]{:T(128)}, /*index=...) while((s32[]{:T(128)}, ...), condition=%wide.region_12.14_spmd.clone, body=%wide.region_7.13_spmd.clone.sunk | while | flops 68168976 | bytes 5054484 | solution.py:78
  24.0 1.6 %collective-permute-start = (bf16[2,256,256]{1,2,0:T(8,128)(2,1)S(1)}, bf16[2,256,256]{1,2,0:T(8,128)(2,1)S(1)}, u32[]{:S(2)}, u32[]{:S(2)}) collective-permute-start(bf16[2,256,256]{1,2,0:T(8,128)(2,1)S(1)} %get-tuple-element.389), channel_id=1, source_target_pairs={{0,4},{4,8},{8,12},{12,16},{16,20},{20,24},{24,28},{28,0},{1,5},{5... | collective-permute-start | bytes 786440 | tf_op jit(solution)/shard_map/while/body/eval_jaxpr/ppermute | solution.py:11
  25.6 0.1 broadcast_in_dim.64
  25.7 1.0 gather_fusion
  26.7 0.8 fusion.35
  28.1 7.4 %collective-permute-done = bf16[2,256,256]{1,2,0:T(8,128)(2,1)S(1)} collective-permute-done((bf16[2,256,256]{1,2,0:T(8,128)(2,1)S(1)}, bf16[2,256,256]{1,2,0:T(8,128)(2,1)S(1)}, u32[]{:S(2)}, u32[]{:S(2)}) %collective-permute-start) | collective-permute-done | bytes 262176 | tf_op jit(solution)/shard_map/while/body/eval_jaxpr/ppermute | solution.py:11
  35.4 0.1 collective-permute-start
  35.6 0.1 broadcast_in_dim.64
  35.7 1.0 gather_fusion
  36.7 0.8 fusion.35
  38.0 8.0 %collective-permute-done = bf16[2,256,256]{1,2,0:T(8,128)(2,1)S(1)} collective-permute-done((bf16[2,256,256]{1,2,0:T(8,128)(2,1)S(1)}, bf16[2,256,256]{1,2,0:T(8,128)(2,1)S(1)}, u32[]{:S(2)}, u32[]{:S(2)}) %collective-permute-start) | collective-permute-done | bytes 262176 | tf_op jit(solution)/shard_map/while/body/eval_jaxpr/ppermute | solution.py:11
  46.1 0.7 conditional.5
  46.1 0.4 fusion.20
  46.6 0.2 fusion.5
  46.8 0.1 collective-permute-start
  47.0 0.1 broadcast_in_dim.64
  47.1 1.0 gather_fusion
  48.0 0.8 fusion.35
  49.4 7.2 %collective-permute-done = bf16[2,256,256]{1,2,0:T(8,128)(2,1)S(1)} collective-permute-done((bf16[2,256,256]{1,2,0:T(8,128)(2,1)S(1)}, bf16[2,256,256]{1,2,0:T(8,128)(2,1)S(1)}, u32[]{:S(2)}, u32[]{:S(2)}) %collective-permute-start) | collective-permute-done | bytes 262176 | tf_op jit(solution)/shard_map/while/body/eval_jaxpr/ppermute | solution.py:11
  56.6 0.1 collective-permute-start
  56.8 0.1 broadcast_in_dim.64
  56.8 1.0 gather_fusion
  57.8 0.8 fusion.35
  59.2 6.5 %collective-permute-done = bf16[2,256,256]{1,2,0:T(8,128)(2,1)S(1)} collective-permute-done((bf16[2,256,256]{1,2,0:T(8,128)(2,1)S(1)}, bf16[2,256,256]{1,2,0:T(8,128)(2,1)S(1)}, u32[]{:S(2)}, u32[]{:S(2)}) %collective-permute-start) | collective-permute-done | bytes 262176 | tf_op jit(solution)/shard_map/while/body/eval_jaxpr/ppermute | solution.py:11
  65.7 0.7 conditional.5
  65.8 0.4 fusion.20
  66.2 0.2 fusion.5
  66.6 0.1 broadcast_in_dim.64
  66.7 1.0 gather_fusion
  67.7 0.8 fusion.35
  69.1 6.5 %collective-permute-done = bf16[2,256,256]{1,2,0:T(8,128)(2,1)S(1)} collective-permute-done((bf16[2,256,256]{1,2,0:T(8,128)(2,1)S(1)}, bf16[2,256,256]{1,2,0:T(8,128)(2,1)S(1)}, u32[]{:S(2)}, u32[]{:S(2)}) %collective-permute-start) | collective-permute-done | bytes 262176 | tf_op jit(solution)/shard_map/while/body/eval_jaxpr/ppermute | solution.py:11
  75.8 0.1 broadcast_in_dim.64
  75.9 1.0 gather_fusion
  76.8 0.8 fusion.35
  78.2 6.5 %collective-permute-done = bf16[2,256,256]{1,2,0:T(8,128)(2,1)S(1)} collective-permute-done((bf16[2,256,256]{1,2,0:T(8,128)(2,1)S(1)}, bf16[2,256,256]{1,2,0:T(8,128)(2,1)S(1)}, u32[]{:S(2)}, u32[]{:S(2)}) %collective-permute-start) | collective-permute-done | bytes 262176 | tf_op jit(solution)/shard_map/while/body/eval_jaxpr/ppermute | solution.py:11
  84.8 0.7 conditional.5
  84.8 0.4 fusion.20
  85.2 0.2 fusion.5
  85.6 0.1 broadcast_in_dim.64
  85.7 1.0 gather_fusion
  86.7 0.8 fusion.35
  88.1 6.5 %collective-permute-done = bf16[2,256,256]{1,2,0:T(8,128)(2,1)S(1)} collective-permute-done((bf16[2,256,256]{1,2,0:T(8,128)(2,1)S(1)}, bf16[2,256,256]{1,2,0:T(8,128)(2,1)S(1)}, u32[]{:S(2)}, u32[]{:S(2)}) %collective-permute-start) | collective-permute-done | bytes 262176 | tf_op jit(solution)/shard_map/while/body/eval_jaxpr/ppermute | solution.py:11
  94.7 1.1 convolution_convert_fusion
  95.8 18.7 %reduce-scatter.2.cloned.1.call-done = bf16[256,256]{1,0:T(8,128)(2,1)} async-done(((bf16[256,1024]{1,0:T(8,128)(2,1)}), bf16[256,256]{1,0:T(8,128)(2,1)}) %reduce-scatter.2.cloned.1.call-update) | async-done | bytes 131088 | tf_op jit(solution)/shard_map/reduce_scatter | solution.py:82
  (77 shorter events, 0.9 us)
Async XLA Ops:
  6.5 88.1 %copy-start = (bf16[256,1024]{1,0:T(8,128)(2,1)S(1)}, bf16[256,1024]{1,0:T(8,128)(2,1)}, u32[]{:S(2)}) copy-start(bf16[256,1024]{1,0:T(8,128)(2,1)} %param.22) | copy-start | bytes 1572868
  6.5 108.0 %reduce-scatter.2.cloned.1.call-start = ((), (), s32[]{:S(2)}) async-start(), calls=%async_computation.1 | async-start | bytes 655360 | tf_op jit(solution)/shard_map/reduce_scatter | solution.py:82
  6.6 0.7 copy-start.7
  6.6 0.7 copy-start.8
  6.6 0.8 copy-start.1
  9.7 1.4 %copy-start.2 = (bf16[256,256]{1,0:T(8,128)(2,1)S(1)}, bf16[256,256]{1,0:T(8,128)(2,1)}, u32[]{:S(2)}) copy-start(bf16[256,256]{1,0:T(8,128)(2,1)} %param.17) | copy-start | bytes 393220
  11.1 9.0 %copy-start.3 = (bf16[1024,256]{1,0:T(8,128)(2,1)S(1)}, bf16[1024,256]{1,0:T(8,128)(2,1)}, u32[]{:S(2)}) copy-start(bf16[1024,256]{1,0:T(8,128)(2,1)} %param.21) | copy-start | bytes 1572868
  19.9 0.7 copy-start.6
  20.6 1.0 copy-start.4
  21.6 1.0 copy-start.5
  24.0 11.4 %collective-permute-start = (bf16[2,256,256]{1,2,0:T(8,128)(2,1)S(1)}, bf16[2,256,256]{1,2,0:T(8,128)(2,1)S(1)}, u32[]{:S(2)}, u32[]{:S(2)}) collective-permute-start(bf16[2,256,256]{1,2,0:T(8,128)(2,1)S(1)} %get-tuple-element.389), channel_id=1, source_target_pairs={{0,4},{4,8},{8,12},{12,16},{16,20},{20,24},{24,28},{28,0},{1,5},{5... | collective-permute-start | bytes 786440 | tf_op jit(solution)/shard_map/while/body/eval_jaxpr/ppermute | solution.py:11
  35.4 10.6 %collective-permute-start = (bf16[2,256,256]{1,2,0:T(8,128)(2,1)S(1)}, bf16[2,256,256]{1,2,0:T(8,128)(2,1)S(1)}, u32[]{:S(2)}, u32[]{:S(2)}) collective-permute-start(bf16[2,256,256]{1,2,0:T(8,128)(2,1)S(1)} %get-tuple-element.389), channel_id=1, source_target_pairs={{0,4},{4,8},{8,12},{12,16},{16,20},{20,24},{24,28},{28,0},{1,5},{5... | collective-permute-start | bytes 786440 | tf_op jit(solution)/shard_map/while/body/eval_jaxpr/ppermute | solution.py:11
  46.8 9.8 %collective-permute-start = (bf16[2,256,256]{1,2,0:T(8,128)(2,1)S(1)}, bf16[2,256,256]{1,2,0:T(8,128)(2,1)S(1)}, u32[]{:S(2)}, u32[]{:S(2)}) collective-permute-start(bf16[2,256,256]{1,2,0:T(8,128)(2,1)S(1)} %get-tuple-element.389), channel_id=1, source_target_pairs={{0,4},{4,8},{8,12},{12,16},{16,20},{20,24},{24,28},{28,0},{1,5},{5... | collective-permute-start | bytes 786440 | tf_op jit(solution)/shard_map/while/body/eval_jaxpr/ppermute | solution.py:11
  56.6 9.1 %collective-permute-start = (bf16[2,256,256]{1,2,0:T(8,128)(2,1)S(1)}, bf16[2,256,256]{1,2,0:T(8,128)(2,1)S(1)}, u32[]{:S(2)}, u32[]{:S(2)}) collective-permute-start(bf16[2,256,256]{1,2,0:T(8,128)(2,1)S(1)} %get-tuple-element.389), channel_id=1, source_target_pairs={{0,4},{4,8},{8,12},{12,16},{16,20},{20,24},{24,28},{28,0},{1,5},{5... | collective-permute-start | bytes 786440 | tf_op jit(solution)/shard_map/while/body/eval_jaxpr/ppermute | solution.py:11
  66.5 9.1 %collective-permute-start = (bf16[2,256,256]{1,2,0:T(8,128)(2,1)S(1)}, bf16[2,256,256]{1,2,0:T(8,128)(2,1)S(1)}, u32[]{:S(2)}, u32[]{:S(2)}) collective-permute-start(bf16[2,256,256]{1,2,0:T(8,128)(2,1)S(1)} %get-tuple-element.389), channel_id=1, source_target_pairs={{0,4},{4,8},{8,12},{12,16},{16,20},{20,24},{24,28},{28,0},{1,5},{5... | collective-permute-start | bytes 786440 | tf_op jit(solution)/shard_map/while/body/eval_jaxpr/ppermute | solution.py:11
  75.6 9.1 %collective-permute-start = (bf16[2,256,256]{1,2,0:T(8,128)(2,1)S(1)}, bf16[2,256,256]{1,2,0:T(8,128)(2,1)S(1)}, u32[]{:S(2)}, u32[]{:S(2)}) collective-permute-start(bf16[2,256,256]{1,2,0:T(8,128)(2,1)S(1)} %get-tuple-element.389), channel_id=1, source_target_pairs={{0,4},{4,8},{8,12},{12,16},{16,20},{20,24},{24,28},{28,0},{1,5},{5... | collective-permute-start | bytes 786440 | tf_op jit(solution)/shard_map/while/body/eval_jaxpr/ppermute | solution.py:11
  85.5 9.1 %collective-permute-start = (bf16[2,256,256]{1,2,0:T(8,128)(2,1)S(1)}, bf16[2,256,256]{1,2,0:T(8,128)(2,1)S(1)}, u32[]{:S(2)}, u32[]{:S(2)}) collective-permute-start(bf16[2,256,256]{1,2,0:T(8,128)(2,1)S(1)} %get-tuple-element.389), channel_id=1, source_target_pairs={{0,4},{4,8},{8,12},{12,16},{16,20},{20,24},{24,28},{28,0},{1,5},{5... | collective-permute-start | bytes 786440 | tf_op jit(solution)/shard_map/while/body/eval_jaxpr/ppermute | solution.py:11
Sparse Core Ops, SparseCore 0:
  95.9 18.4 reduce-scatter.1
where the time goes:
time: 121 us
  waiting for transfers between devices  67.4 us (56%)
  between operations  14.2 us (12%)
  local copies, waits for them, and re-layouts  12.3 us (10%)
  blocking collectives  8.75 us (7%)
  other arithmetic  6.85 us (6%)
  matrix products  5.03 us (4%)
  loops' own time  4.96 us (4%)
  starting transfers between devices  1.92 us (2%)
    ppermute x7, waiting for transfers between devices, shifted(): lax.ppermute(shard, axis, [(i, (i + by) % length) for i in range(length)])  48.7 us
    reduce_scatter x1, waiting for transfers between devices, shards(): lax.psum_scatter(partial_value.astype(jnp.bfloat16), 'head', scatter_dime...  18.7 us
    all_gather x1, blocking collectives, shards(): whole = lax.all_gather(tokens, 'head', axis=1, tiled=True)  8.75 us
    gather x8, local copies, waits for them, and re-layouts, attend(): allowed = (jnp.take(query_live, key_block, axis=1) > 0) & True  7.79 us
    reduce_or x8, other arithmetic, attend(): return lax.cond(jnp.any(allowed), compute, keep, carry)  6.14 us
    another operation x1, loops' own time, shards(): moved, state = lax.fori_loop(0, cycle - 1, turn, (stacked, state))  4.88 us
  transfers between devices with their start and end apart: 8, of which 8 were waited for; matrix products, arithmetic and copies ran while one was open for 11% of the time, Pallas kernels for 0%

commit v1 on v0

v1 whole, which is shorter than its diff:
```python
import functools

import jax
import jax.numpy as jnp
from jax import lax
from jax.experimental import pallas as pl
from jax.experimental.pallas import tpu as pltpu
from jax.sharding import PartitionSpec as P

BLOCK = 128
CHUNKS = 2
EPS = 1e-06
MESH = pl.DeviceIdType.MESH
F32 = jnp.float32
BF16 = jnp.bfloat16


def visit(line, depth, k):
    far = depth - 1 - line
    near = jnp.minimum(line, far)
    both = jnp.where(k % 2 == 1, line - (k + 1) // 2, line + k // 2)
    rest = jnp.where(line < far, line + (k - near), line - (k - near))
    return jnp.where(k <= 2 * near, both, rest)


def kernel(
    depth,
    order_ref, adj_ref, temper_ref, gain_ref, tokens_ref, wq_hbm, wk_hbm, wv_hbm, wo_hbm,
    out_ref,
    tok, wq, wk, wv, wo, mean_mat, kvh, kvr, qh, qr, qm, acc, asend, abuf, part, csend, crecv, xsend, xrecv,
    w_sem, t_sem, zs, zr, xs, xr, cs, cr, ys, yr, qs, qrs, as_, ar, ocs, ocr, oxs, oxr,
):
    ctx, head = lax.axis_index("ctx"), lax.axis_index("head")
    line, y = ctx // 2, ctx % 2
    x, c = head // 2, head % 2
    oy, ox, oc = 1 - y, 1 - x, 1 - c
    rows, cols = tokens_ref.shape
    heads = temper_ref.shape[0]
    width = wq.shape[1]
    size = width // heads
    pair = width // 2
    rp = rows // CHUNKS
    total = depth * CHUNKS
    features = wq.shape[0]
    lag = CHUNKS + 1
    has_left, has_right = line > 0, line < depth - 1
    at_left, at_right = (ctx - 2, head), (ctx + 2, head)
    at_y = (line * 2 + oy, head)
    at_x = (ctx, ox * 2 + c)
    at_c = (ctx, x * 2 + oc)
    xhead = ox * 2 + c
    chead = x * 2 + oc
    dhead = ox * 2 + oc

    def remote(src, dst, send, recv, where):
        return pltpu.make_async_remote_copy(
            src_ref=src, dst_ref=dst, send_sem=send, recv_sem=recv, device_id=where, device_id_type=MESH
        )

    loads = [
        pltpu.make_async_copy(wk_hbm, wk, w_sem.at[0]),
        pltpu.make_async_copy(wv_hbm, wv, w_sem.at[1]),
        pltpu.make_async_copy(wq_hbm, wq, w_sem.at[2]),
    ]
    count = wo.shape[0]
    for h in range(count):
        loads.append(pltpu.make_async_copy(wo_hbm.at[:, pl.ds(h * cols, cols)], wo.at[h], w_sem.at[3 + h]))
    own = [
        pltpu.make_async_copy(tokens_ref.at[pl.ds(j * rp, rp), :], tok.at[line * CHUNKS + j, head], t_sem.at[j])
        for j in range(CHUNKS)
    ]
    for copy in own + loads:
        copy.start()

    barrier = pltpu.get_barrier_semaphore()
    for where in (at_y, at_x, at_c):
        pl.semaphore_signal(barrier, inc=1, device_id=where, device_id_type=MESH)

    @pl.when(has_left)
    def _():
        pl.semaphore_signal(barrier, inc=1, device_id=at_left, device_id_type=MESH)

    @pl.when(has_right)
    def _():
        pl.semaphore_signal(barrier, inc=1, device_id=at_right, device_id_type=MESH)

    row_id = lax.broadcasted_iota(jnp.int32, (width, width), 0) // size
    col_id = lax.broadcasted_iota(jnp.int32, (width, width), 1) // size
    mean_mat[...] = jnp.where(row_id == col_id, 1.0 / size, 0.0).astype(BF16)
    acc[...] = jnp.zeros_like(acc)
    pl.semaphore_wait(barrier, 3 + has_left.astype(jnp.int32) + has_right.astype(jnp.int32))

    def slot_of(n):
        origin = visit(line, depth, n // CHUNKS)
        return origin, origin * CHUNKS + n % CHUNKS

    def z_right(s):
        return remote(tok.at[s, head], tok.at[s, head], zs.at[1, s], zr.at[s], at_right)

    def z_left(s):
        return remote(tok.at[s, head], tok.at[s, head], zs.at[0, s], zr.at[s], at_left)

    def x_copy(s, h):
        return remote(tok.at[s, h], tok.at[s, h], xs.at[s], xr.at[s], at_x)

    def c_copy(s, h, which):
        return remote(tok.at[s, h], tok.at[s, h], cs.at[s, which], cr.at[s, which], at_c)

    def y_copy(s):
        return remote(kvh.at[s, oy], kvr.at[s], ys.at[s], yr.at[s], at_y)

    def q_copy(j):
        return remote(qh.at[oy, j], qr.at[j], qs.at[j], qrs.at[j], at_y)

    def spread(origin, s):
        @pl.when(jnp.logical_and(has_right, origin <= line))
        def _():
            z_right(s).start()

        @pl.when(jnp.logical_and(has_left, origin >= line))
        def _():
            z_left(s).start()

        x_copy(s, head).start()
        c_copy(s, head, 0).start()

    for j in range(CHUNKS):
        own[j].wait()
        spread(line, line * CHUNKS + j)
    for copy in loads:
        copy.wait()

    def unit(values):
        mean = jnp.dot((values * values).astype(BF16), mean_mat[...], preferred_element_type=F32)
        return values * lax.rsqrt(mean + EPS)

    lane_w = lax.broadcasted_iota(jnp.int32, (1, width), 1) // size
    scale = jnp.zeros((1, width), F32)
    for h in range(heads):
        scale = jnp.where(lane_w == h, temper_ref[h] / size, scale)

    def project(n):
        origin, s = slot_of(n)
        c_copy(s, chead, 0).wait_recv()
        c_copy(s, dhead, 1).wait_recv()
        parts = [tok[s, h].astype(F32) for h in range(count)]
        squares = parts[0] * parts[0]
        for p in parts[1:]:
            squares = squares + p * p
        inv = lax.rsqrt(jnp.sum(squares, axis=-1, keepdims=True) * (1.0 / features) + EPS)
        normed = jnp.concatenate(
            [(parts[h] * inv * gain_ref[:, h * cols:(h + 1) * cols]).astype(BF16) for h in range(count)], axis=1
        )
        keys = unit(jnp.dot(normed, wk[...], preferred_element_type=F32)).astype(BF16)
        values = jnp.dot(normed, wv[...], preferred_element_type=F32).astype(BF16)
        for half in range(2):
            kvh[s, half, 0] = keys[:, half * pair:(half + 1) * pair]
            kvh[s, half, 1] = values[:, half * pair:(half + 1) * pair]
        y_copy(s).start()

        @pl.when(n < CHUNKS)
        def _():
            query = unit(jnp.dot(normed, wq[...], preferred_element_type=F32))
            query = (query * scale).astype(BF16)
            for half in range(2):
                qh[half, n] = query[:, half * pair:(half + 1) * pair]
            q_copy(n).start()

    low = lax.broadcasted_iota(jnp.int32, (1, pair), 1) < size

    def split_queries():
        for j in range(CHUNKS):
            q_copy(j).wait_recv()
        for side in range(2):
            for j in range(CHUNKS):
                piece = qh[y, j] if side == 0 else qr[j]
                at = side * rows + j * rp
                zero = jnp.zeros_like(piece)
                qm[0, at:at + rp, :] = jnp.where(low, piece, zero)
                qm[1, at:at + rp, :] = jnp.where(low, zero, piece)

    local = rows // BLOCK
    per_chunk = rp // BLOCK
    q_blocks = [order_ref[(line * 2 + side) * local + i] for side in (y, oy) for i in range(local)]
    key_lane = lax.broadcasted_iota(jnp.int32, (1, 2 * rp), 1) // BLOCK

    def attend(n):
        origin, s = slot_of(n)
        y_copy(s).wait_recv()
        keys = jnp.concatenate([kvh[s, y, 0], kvr[s, 0]], axis=0)
        values = jnp.concatenate([kvh[s, y, 1], kvr[s, 1]], axis=0)
        first = (n % CHUNKS) * per_chunk
        k_blocks = [order_ref[(origin * 2 + side) * local + first + i] for side in (y, oy) for i in range(per_chunk)]
        masks = []
        for qb in q_blocks:
            mask = jnp.zeros((1, 2 * rp), F32)
            for i, kb in enumerate(k_blocks):
                mask = jnp.where(key_lane == i, (adj_ref[qb, kb] > 0).astype(F32), mask)
            masks.append(mask)
        ones = jnp.ones_like(values)
        for h in range(2):
            mine = jnp.where(low, values, ones) if h == 0 else jnp.where(low, ones, values)
            scores = lax.dot_general(qm[h], keys, (((1,), (1,)), ((), ())), preferred_element_type=F32)
            probs = jnp.concatenate(
                [(jnp.exp(scores[i * BLOCK:(i + 1) * BLOCK]) * masks[i]).astype(BF16) for i in range(2 * local)], axis=0
            )
            acc[h] += jnp.dot(probs, mine, preferred_element_type=F32)

    def step(n, carry):
        @pl.when(n + CHUNKS < total)
        def _():
            origin, s = slot_of(n + CHUNKS)
            z_left(s).wait_recv()
            spread(origin, s)

        @pl.when(n < total)
        def _():
            origin, s = slot_of(n)
            x_copy(s, xhead).wait_recv()
            c_copy(s, xhead, 1).start()

        @pl.when(jnp.logical_and(n >= 1, n <= total))
        def _():
            project(n - 1)

        @pl.when(n == lag)
        def _():
            split_queries()

        @pl.when(n >= lag)
        def _():
            attend(n - lag)

        return carry

    lax.fori_loop(0, total + lag, step, 0)

    top = jnp.where(low, acc[0], acc[1])
    weight = pltpu.roll(jnp.where(low, acc[1], acc[0]), size, 1)
    attended = (top / weight).astype(BF16)
    asend[...] = attended[rows:]
    a_copy = remote(asend, abuf.at[y], as_, ar, at_y)
    a_copy.start()
    abuf[y] = attended[:rows]
    remote(asend, abuf.at[oy], as_, ar, at_y).wait_recv()

    c_outs, x_outs = [], []
    for r in range(CHUNKS):
        at = r * rp
        feats = jnp.concatenate([abuf[0, at:at + rp, :], abuf[1, at:at + rp, :]], axis=1)
        csend[r, 0] = jnp.dot(feats, wo[dhead], preferred_element_type=F32).astype(BF16)
        csend[r, 1] = jnp.dot(feats, wo[chead], preferred_element_type=F32).astype(BF16)
        c_out = remote(csend.at[r], crecv.at[r], ocs.at[r], ocr.at[r], at_c)
        c_out.start()
        c_outs.append(c_out)
        part[r, 0] = jnp.dot(feats, wo[xhead], preferred_element_type=F32)
        part[r, 1] = jnp.dot(feats, wo[head], preferred_element_type=F32)
    for r in range(CHUNKS):
        c_outs[r].wait_recv()
        xsend[r] = (part[r, 0] + crecv[r, 0].astype(F32)).astype(BF16)
        x_out = remote(xsend.at[r], xrecv.at[r], oxs.at[r], oxr.at[r], at_x)
        x_out.start()
        x_outs.append(x_out)
    for r in range(CHUNKS):
        x_outs[r].wait_recv()
        whole = part[r, 1] + crecv[r, 1].astype(F32) + xrecv[r].astype(F32)
        out_ref[r * rp:(r + 1) * rp, :] = whole.astype(BF16)

    def drain(n, carry):
        origin, s = slot_of(n)

        @pl.when(jnp.logical_and(has_right, origin <= line))
        def _():
            z_right(s).wait_send()

        @pl.when(jnp.logical_and(has_left, origin >= line))
        def _():
            z_left(s).wait_send()

        x_copy(s, head).wait_send()
        c_copy(s, head, 0).wait_send()
        c_copy(s, xhead, 1).wait_send()
        y_copy(s).wait_send()
        return carry

    lax.fori_loop(0, total, drain, 0)
    for j in range(CHUNKS):
        q_copy(j).wait_send()
        c_outs[j].wait_send()
        x_outs[j].wait_send()
    a_copy.wait_send()


def shards(depth, tokens, gain, w_query, w_key, w_value, w_out, temper, adjacency, order):
    rows, cols = tokens.shape
    features, width = w_query.shape
    count = features // cols
    pair = width // 2
    rp = rows // CHUNKS
    total = depth * CHUNKS
    dma = pltpu.SemaphoreType.DMA
    smem = pl.BlockSpec(memory_space=pltpu.SMEM)
    vmem = pl.BlockSpec(memory_space=pltpu.VMEM)
    hbm = pl.BlockSpec(memory_space=pl.ANY)
    return pl.pallas_call(
        functools.partial(kernel, depth),
        out_shape=jax.ShapeDtypeStruct((rows, cols), BF16),
        in_specs=[smem, smem, smem, vmem, hbm, hbm, hbm, hbm, hbm],
        out_specs=vmem,
        scratch_shapes=[
            pltpu.VMEM((total, count, rp, cols), BF16),
            pltpu.VMEM((features, width), BF16),
            pltpu.VMEM((features, width), BF16),
            pltpu.VMEM((features, width), BF16),
            pltpu.VMEM((count, width, cols), BF16),
            pltpu.VMEM((width, width), BF16),
            pltpu.VMEM((total, 2, 2, rp, pair), BF16),
            pltpu.VMEM((total, 2, rp, pair), BF16),
            pltpu.VMEM((2, CHUNKS, rp, pair), BF16),
            pltpu.VMEM((CHUNKS, rp, pair), BF16),
            pltpu.VMEM((2, 2 * rows, pair), BF16),
            pltpu.VMEM((2, 2 * rows, pair), F32),
            pltpu.VMEM((rows, pair), BF16),
            pltpu.VMEM((2, rows, pair), BF16),
            pltpu.VMEM((CHUNKS, 2, rp, cols), F32),
            pltpu.VMEM((CHUNKS, 2, rp, cols), BF16),
            pltpu.VMEM((CHUNKS, 2, rp, cols), BF16),
            pltpu.VMEM((CHUNKS, rp, cols), BF16),
            pltpu.VMEM((CHUNKS, rp, cols), BF16),
            dma((3 + count,)),
            dma((CHUNKS,)),
            dma((2, total)),
            dma((total,)),
            dma((total,)),
            dma((total,)),
            dma((total, 2)),
            dma((total, 2)),
            dma((total,)),
            dma((total,)),
            dma((CHUNKS,)),
            dma((CHUNKS,)),
            dma,
            dma,
            dma((CHUNKS,)),
            dma((CHUNKS,)),
            dma((CHUNKS,)),
            dma((CHUNKS,)),
        ],
        compiler_params=pltpu.CompilerParams(
            collective_id=0, has_side_effects=True, vmem_limit_bytes=56 * 1024 * 1024
        ),
    )(order, adjacency, temper, gain.reshape(1, features), tokens, w_query, w_key, w_value, w_out)


def solution(mesh):
    in_specs = (
        P("ctx", "head"),
        P(),
        P(None, "head"),
        P(None, "head"),
        P(None, "head"),
        P("head", None),
        P("head"),
        P(),
        P(),
    )
    out_specs = P("ctx", "head")
    body = functools.partial(shards, mesh.shape["ctx"] // 2)
    return jax.shard_map(body, mesh=mesh, in_specs=in_specs, out_specs=out_specs, check_vma=False)
```

time: 121 us -> 45.2 us (0.37)
  waiting for transfers between devices: 67.4 us -> 0 us
  Pallas kernels: 0 us -> 43.4 us
  between operations: 14.2 us -> 0.01 us
  local copies, waits for them, and re-layouts: 12.3 us -> 1.57 us
  blocking collectives: 8.75 us -> 0 us
  other arithmetic: 6.85 us -> 0 us
  matrix products: 5.03 us -> 0 us
  loops' own time: 4.96 us -> 0 us
  starting transfers between devices: 1.92 us -> 0 us
    ppermute x7 -> x0, waiting for transfers between devices: 48.7 us -> none  [shifted(): lax.ppermute(shard, axis, [(i, (i + by) % length) for i in range(length)])]
    pallas_call x0 -> x1, Pallas kernels: none -> 43.4 us  [shards(): pl.pallas_call(functools.partial(kernel, depth), out_shape=jax.ShapeDtype...]
    reduce_scatter x1 -> x0, waiting for transfers between devices: 18.7 us -> none  [shards(): lax.psum_scatter(partial_value.astype(jnp.bfloat16), 'head', scatter_dime...]
    gather x11 -> x0, local copies, waits for them, and re-layouts: 8.98 us -> none  [the longest x8 7.79 us: attend(): allowed = (jnp.take(query_live, key_block, axis=1) > 0) & True]
    all_gather x1 -> x0, blocking collectives: 8.75 us -> none  [shards(): whole = lax.all_gather(tokens, 'head', axis=1, tiled=True)]
    reduce_or x8 -> x0, other arithmetic: 6.14 us -> none  [attend(): return lax.cond(jnp.any(allowed), compute, keep, carry)]
    dot_general x12 -> x0, matrix products: 5.03 us -> none  [the longest x4 1.68 us: compute(): jnp.einsum('qhd,khd->hqk', query, keys_piece, preferred_element_type=jnp....]
    another operation x9 -> x0, loops' own time: 4.96 us -> none  [the longest x1 4.88 us: shards(): moved, state = lax.fori_loop(0, cycle - 1, turn, (stacked, state))]
  transfers between devices with their start and end apart: 8 -> 0, of which waited for: 8 -> 0; matrix products, arithmetic and copies ran while one was open for 11% -> 0% of each run, Pallas kernels for 0% -> 0%
where the time goes in v1:
time: 45.2 us; the launch traced here: 45 us
  Pallas kernels  43.4 us (96%)
  local copies, waits for them, and re-layouts  1.57 us (3%)
    pallas_call x1, Pallas kernels, shards(): pl.pallas_call(functools.partial(kernel, depth), out_shape=jax.ShapeDtype...  43.4 us
    unnamed x1, local copies, waits for them, and re-layouts  1.57 us

profile of v1, /device:TPU:0, one launch (start us, length us, event | category | flops | bytes accessed | tf_op | source)
XLA Modules:
  0.0 45.0 jit_solution(16253206500857390222)
XLA Ops:
  0.0 43.4 %shard_map.91 = bf16[256,256]{1,0:T(8,128)(2,1)} custom-call(s32[16]{0:T(128)} %order_ref.1, s32[16,16]{1,0:T(8,128)} %adj_ref.1, f32[4]{0:T(128)} %temper_ref.1, f32[1,1024]{1,0:T(1,128)} %bitcast.1, bf16[256,256]{1,0:T(8,128)(2,1)} %tokens_ref.1, bf16[1024,256]{1,0:T(8,128)(2,1)} %wq_hbm.1, bf16[1024,256]{1,0:T(8,128)(2,1)} %wk_hbm.1, ...), custom_call_target="tpu_custom_call" | custom-call | tf_op jit(solution)/shard_map/pallas_call | solution.py:305
  43.4 1.6 %copy.11 = bf16[256,256]{1,0:T(8,128)(2,1)} copy(bf16[256,256]{1,0:T(8,128)(2,1)} %shard_map.91) | data formatting | bytes 262144

commit v2 on v1

--- a/solution.py
+++ b/solution.py
@@ -15,12 +15,16 @@
 BF16 = jnp.bfloat16
 
 
-def visit(line, depth, k):
+def visit(line, depth, n):
     far = depth - 1 - line
-    near = jnp.minimum(line, far)
-    both = jnp.where(k % 2 == 1, line - (k + 1) // 2, line + k // 2)
-    rest = jnp.where(line < far, line + (k - near), line - (k - near))
-    return jnp.where(k <= 2 * near, both, rest)
+    near = jnp.minimum(line, far) * CHUNKS
+    p = n - CHUNKS
+    paired = p < 2 * near
+    t = jnp.where(paired, p // 2, p - near)
+    to_left = jnp.where(paired, p % 2 == 0, line > far)
+    away = t // CHUNKS + 1
+    origin = jnp.where(n < CHUNKS, line, jnp.where(to_left, line - away, line + away))
+    return origin, jnp.where(n < CHUNKS, n, t % CHUNKS)
 
 
 def kernel(
@@ -91,8 +95,8 @@
     pl.semaphore_wait(barrier, 3 + has_left.astype(jnp.int32) + has_right.astype(jnp.int32))
 
     def slot_of(n):
-        origin = visit(line, depth, n // CHUNKS)
-        return origin, origin * CHUNKS + n % CHUNKS
+        origin, j = visit(line, depth, n)
+        return origin, origin * CHUNKS + j
 
     def z_right(s):
         return remote(tok.at[s, head], tok.at[s, head], zs.at[1, s], zr.at[s], at_right)
@@ -127,7 +131,7 @@
     for j in range(CHUNKS):
         own[j].wait()
         spread(line, line * CHUNKS + j)
-    for copy in loads:
+    for copy in loads[:3]:
         copy.wait()
 
     def unit(values):
@@ -189,7 +193,7 @@
         y_copy(s).wait_recv()
         keys = jnp.concatenate([kvh[s, y, 0], kvr[s, 0]], axis=0)
         values = jnp.concatenate([kvh[s, y, 1], kvr[s, 1]], axis=0)
-        first = (n % CHUNKS) * per_chunk
+        first = (s - origin * CHUNKS) * per_chunk
         k_blocks = [order_ref[(origin * 2 + side) * local + first + i] for side in (y, oy) for i in range(per_chunk)]
         masks = []
         for qb in q_blocks:
@@ -207,11 +211,19 @@
             acc[h] += jnp.dot(probs, mine, preferred_element_type=F32)
 
     def step(n, carry):
-        @pl.when(n + CHUNKS < total)
-        def _():
-            origin, s = slot_of(n + CHUNKS)
+        away = n // CHUNKS + 1
+
+        @pl.when(line - away >= 0)
+        def _():
+            s = (line - away) * CHUNKS + n % CHUNKS
+            z_right(s).wait_recv()
+            spread(line - away, s)
+
+        @pl.when(line + away < depth)
+        def _():
+            s = (line + away) * CHUNKS + n % CHUNKS
             z_left(s).wait_recv()
-            spread(origin, s)
+            spread(line + away, s)
 
         @pl.when(n < total)
         def _():
@@ -235,33 +247,43 @@
 
     lax.fori_loop(0, total + lag, step, 0)
 
-    top = jnp.where(low, acc[0], acc[1])
-    weight = pltpu.roll(jnp.where(low, acc[1], acc[0]), size, 1)
-    attended = (top / weight).astype(BF16)
-    asend[...] = attended[rows:]
-    a_copy = remote(asend, abuf.at[y], as_, ar, at_y)
-    a_copy.start()
-    abuf[y] = attended[:rows]
-    remote(asend, abuf.at[oy], as_, ar, at_y).wait_recv()
-
-    c_outs, x_outs = [], []
-    for r in range(CHUNKS):
-        at = r * rp
-        feats = jnp.concatenate([abuf[0, at:at + rp, :], abuf[1, at:at + rp, :]], axis=1)
+    def finish(at):
+        first, second = acc[0, at:at + rp, :], acc[1, at:at + rp, :]
+        weight = pltpu.roll(jnp.where(low, second, first), size, 1)
+        return (jnp.where(low, first, second) / weight).astype(BF16)
+
+    def a_copy(r):
+        return remote(asend.at[r], abuf.at[y, r], as_.at[r], ar.at[r], at_y)
+
+    for r in range(CHUNKS):
+        asend[r] = finish(rows + r * rp)
+        a_copy(r).start()
+    for r in range(CHUNKS):
+        abuf[y, r] = finish(r * rp)
+    for copy in loads[3:]:
+        copy.wait()
+
+    def c_out(r, which):
+        return remote(csend.at[r, which], crecv.at[r, which], ocs.at[r, which], ocr.at[r, which], at_c)
+
+    x_outs = []
+    for r in range(CHUNKS):
+        a_copy(r).wait_recv()
+        feats = jnp.concatenate([abuf[0, r], abuf[1, r]], axis=1)
         csend[r, 0] = jnp.dot(feats, wo[dhead], preferred_element_type=F32).astype(BF16)
+        c_out(r, 0).start()
+        part[r, 0] = jnp.dot(feats, wo[xhead], preferred_element_type=F32)
         csend[r, 1] = jnp.dot(feats, wo[chead], preferred_element_type=F32).astype(BF16)
-        c_out = remote(csend.at[r], crecv.at[r], ocs.at[r], ocr.at[r], at_c)
-        c_out.start()
-        c_outs.append(c_out)
-        part[r, 0] = jnp.dot(feats, wo[xhead], preferred_element_type=F32)
+        c_out(r, 1).start()
         part[r, 1] = jnp.dot(feats, wo[head], preferred_element_type=F32)
     for r in range(CHUNKS):
-        c_outs[r].wait_recv()
+        c_out(r, 0).wait_recv()
         xsend[r] = (part[r, 0] + crecv[r, 0].astype(F32)).astype(BF16)
         x_out = remote(xsend.at[r], xrecv.at[r], oxs.at[r], oxr.at[r], at_x)
         x_out.start()
         x_outs.append(x_out)
     for r in range(CHUNKS):
+        c_out(r, 1).wait_recv()
         x_outs[r].wait_recv()
         whole = part[r, 1] + crecv[r, 1].astype(F32) + xrecv[r].astype(F32)
         out_ref[r * rp:(r + 1) * rp, :] = whole.astype(BF16)
@@ -286,9 +308,10 @@
     lax.fori_loop(0, total, drain, 0)
     for j in range(CHUNKS):
         q_copy(j).wait_send()
-        c_outs[j].wait_send()
+        c_out(j, 0).wait_send()
+        c_out(j, 1).wait_send()
         x_outs[j].wait_send()
-    a_copy.wait_send()
+        a_copy(j).wait_send()
 
 
 def shards(depth, tokens, gain, w_query, w_key, w_value, w_out, temper, adjacency, order):
@@ -320,8 +343,8 @@
             pltpu.VMEM((CHUNKS, rp, pair), BF16),
             pltpu.VMEM((2, 2 * rows, pair), BF16),
             pltpu.VMEM((2, 2 * rows, pair), F32),
-            pltpu.VMEM((rows, pair), BF16),
-            pltpu.VMEM((2, rows, pair), BF16),
+            pltpu.VMEM((CHUNKS, rp, pair), BF16),
+            pltpu.VMEM((2, CHUNKS, rp, pair), BF16),
             pltpu.VMEM((CHUNKS, 2, rp, cols), F32),
             pltpu.VMEM((CHUNKS, 2, rp, cols), BF16),
             pltpu.VMEM((CHUNKS, 2, rp, cols), BF16),
@@ -339,10 +362,10 @@
             dma((total,)),
             dma((CHUNKS,)),
             dma((CHUNKS,)),
-            dma,
-            dma,
-            dma((CHUNKS,)),
-            dma((CHUNKS,)),
+            dma((CHUNKS,)),
+            dma((CHUNKS,)),
+            dma((CHUNKS, 2)),
+            dma((CHUNKS, 2)),
             dma((CHUNKS,)),
             dma((CHUNKS,)),
         ],

time: 45.2 us -> 41.1 us (0.909)
  Pallas kernels: 43.4 us -> 39.3 us
    pallas_call x1, Pallas kernels: 43.4 us -> 39.3 us  [shards(): pl.pallas_call(functools.partial(kernel, depth), out_shape=jax.ShapeDtype...]
where the time goes in v2:
time: 41.1 us; the launch traced here: 40.9 us
  Pallas kernels  39.3 us (96%)
  local copies, waits for them, and re-layouts  1.57 us (4%)
    pallas_call x1, Pallas kernels, shards(): pl.pallas_call(functools.partial(kernel, depth), out_shape=jax.ShapeDtype...  39.3 us
    unnamed x1, local copies, waits for them, and re-layouts  1.57 us

profile of v2, /device:TPU:0, one launch (start us, length us, event | category | flops | bytes accessed | tf_op | source)
XLA Modules:
  0.0 40.9 jit_solution(12364257577958109800)
XLA Ops:
  0.0 39.3 %shard_map.91 = bf16[256,256]{1,0:T(8,128)(2,1)} custom-call(s32[16]{0:T(128)} %order_ref.1, s32[16,16]{1,0:T(8,128)} %adj_ref.1, f32[4]{0:T(128)} %temper_ref.1, f32[1,1024]{1,0:T(1,128)} %bitcast.1, bf16[256,256]{1,0:T(8,128)(2,1)} %tokens_ref.1, bf16[1024,256]{1,0:T(8,128)(2,1)} %wq_hbm.1, bf16[1024,256]{1,0:T(8,128)(2,1)} %wk_hbm.1, ...), custom_call_target="tpu_custom_call" | custom-call | tf_op jit(solution)/shard_map/pallas_call | solution.py:328
  39.3 1.6 %copy.11 = bf16[256,256]{1,0:T(8,128)(2,1)} copy(bf16[256,256]{1,0:T(8,128)(2,1)} %shard_map.91) | data formatting | bytes 262144

commit v3 on v2

--- a/solution.py
+++ b/solution.py
@@ -8,8 +8,10 @@
 from jax.sharding import PartitionSpec as P
 
 BLOCK = 128
-CHUNKS = 2
+CHUNKS = 1
+TAIL = 2
 EPS = 1e-06
+LOG2E = 1.4426950408889634
 MESH = pl.DeviceIdType.MESH
 F32 = jnp.float32
 BF16 = jnp.bfloat16
@@ -141,7 +143,7 @@
     lane_w = lax.broadcasted_iota(jnp.int32, (1, width), 1) // size
     scale = jnp.zeros((1, width), F32)
     for h in range(heads):
-        scale = jnp.where(lane_w == h, temper_ref[h] / size, scale)
+        scale = jnp.where(lane_w == h, temper_ref[h] * (LOG2E / size), scale)
 
     def project(n):
         origin, s = slot_of(n)
@@ -206,7 +208,7 @@
             mine = jnp.where(low, values, ones) if h == 0 else jnp.where(low, ones, values)
             scores = lax.dot_general(qm[h], keys, (((1,), (1,)), ((), ())), preferred_element_type=F32)
             probs = jnp.concatenate(
-                [(jnp.exp(scores[i * BLOCK:(i + 1) * BLOCK]) * masks[i]).astype(BF16) for i in range(2 * local)], axis=0
+                [(jnp.exp2(scores[i * BLOCK:(i + 1) * BLOCK]) * masks[i]).astype(BF16) for i in range(2 * local)], axis=0
             )
             acc[h] += jnp.dot(probs, mine, preferred_element_type=F32)
 
@@ -247,19 +249,21 @@
 
     lax.fori_loop(0, total + lag, step, 0)
 
+    tp = rows // TAIL
+
     def finish(at):
-        first, second = acc[0, at:at + rp, :], acc[1, at:at + rp, :]
+        first, second = acc[0, at:at + tp, :], acc[1, at:at + tp, :]
         weight = pltpu.roll(jnp.where(low, second, first), size, 1)
         return (jnp.where(low, first, second) / weight).astype(BF16)
 
     def a_copy(r):
         return remote(asend.at[r], abuf.at[y, r], as_.at[r], ar.at[r], at_y)
 
-    for r in range(CHUNKS):
-        asend[r] = finish(rows + r * rp)
+    for r in range(TAIL):
+        asend[r] = finish(rows + r * tp)
         a_copy(r).start()
-    for r in range(CHUNKS):
-        abuf[y, r] = finish(r * rp)
+    for r in range(TAIL):
+        abuf[y, r] = finish(r * tp)
     for copy in loads[3:]:
         copy.wait()
 
@@ -267,7 +271,7 @@
         return remote(csend.at[r, which], crecv.at[r, which], ocs.at[r, which], ocr.at[r, which], at_c)
 
     x_outs = []
-    for r in range(CHUNKS):
+    for r in range(TAIL):
         a_copy(r).wait_recv()
         feats = jnp.concatenate([abuf[0, r], abuf[1, r]], axis=1)
         csend[r, 0] = jnp.dot(feats, wo[dhead], preferred_element_type=F32).astype(BF16)
@@ -276,17 +280,17 @@
         csend[r, 1] = jnp.dot(feats, wo[chead], preferred_element_type=F32).astype(BF16)
         c_out(r, 1).start()
         part[r, 1] = jnp.dot(feats, wo[head], preferred_element_type=F32)
-    for r in range(CHUNKS):
+    for r in range(TAIL):
         c_out(r, 0).wait_recv()
         xsend[r] = (part[r, 0] + crecv[r, 0].astype(F32)).astype(BF16)
         x_out = remote(xsend.at[r], xrecv.at[r], oxs.at[r], oxr.at[r], at_x)
         x_out.start()
         x_outs.append(x_out)
-    for r in range(CHUNKS):
+    for r in range(TAIL):
         c_out(r, 1).wait_recv()
         x_outs[r].wait_recv()
         whole = part[r, 1] + crecv[r, 1].astype(F32) + xrecv[r].astype(F32)
-        out_ref[r * rp:(r + 1) * rp, :] = whole.astype(BF16)
+        out_ref[r * tp:(r + 1) * tp, :] = whole.astype(BF16)
 
     def drain(n, carry):
         origin, s = slot_of(n)
@@ -308,6 +312,7 @@
     lax.fori_loop(0, total, drain, 0)
     for j in range(CHUNKS):
         q_copy(j).wait_send()
+    for j in range(TAIL):
         c_out(j, 0).wait_send()
         c_out(j, 1).wait_send()
         x_outs[j].wait_send()
@@ -320,6 +325,7 @@
     count = features // cols
     pair = width // 2
     rp = rows // CHUNKS
+    tp = rows // TAIL
     total = depth * CHUNKS
     dma = pltpu.SemaphoreType.DMA
     smem = pl.BlockSpec(memory_space=pltpu.SMEM)
@@ -343,13 +349,13 @@
             pltpu.VMEM((CHUNKS, rp, pair), BF16),
             pltpu.VMEM((2, 2 * rows, pair), BF16),
             pltpu.VMEM((2, 2 * rows, pair), F32),
-            pltpu.VMEM((CHUNKS, rp, pair), BF16),
-            pltpu.VMEM((2, CHUNKS, rp, pair), BF16),
-            pltpu.VMEM((CHUNKS, 2, rp, cols), F32),
-            pltpu.VMEM((CHUNKS, 2, rp, cols), BF16),
-            pltpu.VMEM((CHUNKS, 2, rp, cols), BF16),
-            pltpu.VMEM((CHUNKS, rp, cols), BF16),
-            pltpu.VMEM((CHUNKS, rp, cols), BF16),
+            pltpu.VMEM((TAIL, tp, pair), BF16),
+            pltpu.VMEM((2, TAIL, tp, pair), BF16),
+            pltpu.VMEM((TAIL, 2, tp, cols), F32),
+            pltpu.VMEM((TAIL, 2, tp, cols), BF16),
+            pltpu.VMEM((TAIL, 2, tp, cols), BF16),
+            pltpu.VMEM((TAIL, tp, cols), BF16),
+            pltpu.VMEM((TAIL, tp, cols), BF16),
             dma((3 + count,)),
             dma((CHUNKS,)),
             dma((2, total)),
@@ -362,12 +368,12 @@
             dma((total,)),
             dma((CHUNKS,)),
             dma((CHUNKS,)),
-            dma((CHUNKS,)),
-            dma((CHUNKS,)),
-            dma((CHUNKS, 2)),
-            dma((CHUNKS, 2)),
-            dma((CHUNKS,)),
-            dma((CHUNKS,)),
+            dma((TAIL,)),
+            dma((TAIL,)),
+            dma((TAIL, 2)),
+            dma((TAIL, 2)),
+            dma((TAIL,)),
+            dma((TAIL,)),
         ],
         compiler_params=pltpu.CompilerParams(
             collective_id=0, has_side_effects=True, vmem_limit_bytes=56 * 1024 * 1024

time: 41.1 us -> 43 us (1.046)
  Pallas kernels: 39.3 us -> 41.2 us
    pallas_call x1, Pallas kernels: 39.3 us -> 41.2 us  [shards(): pl.pallas_call(functools.partial(kernel, depth), out_shape=jax.ShapeDtype...]
where the time goes in v3:
time: 43 us; the launch traced here: 42.8 us
  Pallas kernels  41.2 us (96%)
  local copies, waits for them, and re-layouts  1.57 us (4%)
    pallas_call x1, Pallas kernels, shards(): pl.pallas_call(functools.partial(kernel, depth), out_shape=jax.ShapeDtype...  41.2 us
    unnamed x1, local copies, waits for them, and re-layouts  1.57 us

profile of v3, /device:TPU:0, one launch (start us, length us, event | category | flops | bytes accessed | tf_op | source)
XLA Modules:
  0.0 42.8 jit_solution(6139701258765405888)
XLA Ops:
  0.0 41.2 %shard_map.91 = bf16[256,256]{1,0:T(8,128)(2,1)} custom-call(s32[16]{0:T(128)} %order_ref.1, s32[16,16]{1,0:T(8,128)} %adj_ref.1, f32[4]{0:T(128)} %temper_ref.1, f32[1,1024]{1,0:T(1,128)} %bitcast.1, bf16[256,256]{1,0:T(8,128)(2,1)} %tokens_ref.1, bf16[1024,256]{1,0:T(8,128)(2,1)} %wq_hbm.1, bf16[1024,256]{1,0:T(8,128)(2,1)} %wk_hbm.1, ...), custom_call_target="tpu_custom_call" | custom-call | tf_op jit(solution)/shard_map/pallas_call | solution.py:334
  41.2 1.6 %copy.11 = bf16[256,256]{1,0:T(8,128)(2,1)} copy(bf16[256,256]{1,0:T(8,128)(2,1)} %shard_map.91) | data formatting | bytes 262144

commit v4 on v3

--- a/solution.py
+++ b/solution.py
@@ -8,7 +8,7 @@
 from jax.sharding import PartitionSpec as P
 
 BLOCK = 128
-CHUNKS = 1
+CHUNKS = 2
 TAIL = 2
 EPS = 1e-06
 LOG2E = 1.4426950408889634
@@ -32,9 +32,9 @@
 def kernel(
     depth,
     order_ref, adj_ref, temper_ref, gain_ref, tokens_ref, wq_hbm, wk_hbm, wv_hbm, wo_hbm,
-    out_ref,
-    tok, wq, wk, wv, wo, mean_mat, kvh, kvr, qh, qr, qm, acc, asend, abuf, part, csend, crecv, xsend, xrecv,
-    w_sem, t_sem, zs, zr, xs, xr, cs, cr, ys, yr, qs, qrs, as_, ar, ocs, ocr, oxs, oxr,
+    all_ref, wall_ref,
+    tok, wq, wk, wv, mean_mat, kvh, kvr, qh, qr, qm, acc, asend, abuf, xbuf,
+    w_sem, t_sem, zs, zr, xs, xr, cs, cr, ys, yr, qs, qrs, as_, ar, axs, axr, acs, acr, al, ws, wr, wl,
 ):
     ctx, head = lax.axis_index("ctx"), lax.axis_index("head")
     line, y = ctx // 2, ctx % 2
@@ -57,6 +57,7 @@
     xhead = ox * 2 + c
     chead = x * 2 + oc
     dhead = ox * 2 + oc
+    at_d = (ctx, dhead)
 
     def remote(src, dst, send, recv, where):
         return pltpu.make_async_remote_copy(
@@ -68,9 +69,7 @@
         pltpu.make_async_copy(wv_hbm, wv, w_sem.at[1]),
         pltpu.make_async_copy(wq_hbm, wq, w_sem.at[2]),
     ]
-    count = wo.shape[0]
-    for h in range(count):
-        loads.append(pltpu.make_async_copy(wo_hbm.at[:, pl.ds(h * cols, cols)], wo.at[h], w_sem.at[3 + h]))
+    count = features // cols
     own = [
         pltpu.make_async_copy(tokens_ref.at[pl.ds(j * rp, rp), :], tok.at[line * CHUNKS + j, head], t_sem.at[j])
         for j in range(CHUNKS)
@@ -79,7 +78,7 @@
         copy.start()
 
     barrier = pltpu.get_barrier_semaphore()
-    for where in (at_y, at_x, at_c):
+    for where in (at_y, at_x, at_c, at_d):
         pl.semaphore_signal(barrier, inc=1, device_id=where, device_id_type=MESH)
 
     @pl.when(has_left)
@@ -94,7 +93,7 @@
     col_id = lax.broadcasted_iota(jnp.int32, (width, width), 1) // size
     mean_mat[...] = jnp.where(row_id == col_id, 1.0 / size, 0.0).astype(BF16)
     acc[...] = jnp.zeros_like(acc)
-    pl.semaphore_wait(barrier, 3 + has_left.astype(jnp.int32) + has_right.astype(jnp.int32))
+    pl.semaphore_wait(barrier, 4 + has_left.astype(jnp.int32) + has_right.astype(jnp.int32))
 
     def slot_of(n):
         origin, j = visit(line, depth, n)
@@ -133,7 +132,7 @@
     for j in range(CHUNKS):
         own[j].wait()
         spread(line, line * CHUNKS + j)
-    for copy in loads[:3]:
+    for copy in loads:
         copy.wait()
 
     def unit(values):
@@ -212,6 +211,19 @@
             )
             acc[h] += jnp.dot(probs, mine, preferred_element_type=F32)
 
+    def w_columns(h):
+        return wo_hbm.at[:, pl.ds(pl.multiple_of(h * cols, cols), cols)]
+
+    def w_rows(h):
+        return wall_ref.at[pl.ds(pl.multiple_of(h * width, width), width), :]
+
+    def w_copy(which):
+        h, where = ((xhead, at_x), (dhead, at_d), (chead, at_c))[which]
+        return remote(w_columns(h), w_rows(head), ws.at[which], wr.at[which], where)
+
+    def w_own():
+        return pltpu.make_async_copy(w_columns(head), w_rows(head), wl)
+
     def step(n, carry):
         away = n // CHUNKS + 1
 
@@ -232,6 +244,12 @@
             origin, s = slot_of(n)
             x_copy(s, xhead).wait_recv()
             c_copy(s, xhead, 1).start()
+
+        @pl.when(n == total - 1)
+        def _():
+            for which in range(3):
+                w_copy(which).start()
+            w_own().start()
 
         @pl.when(jnp.logical_and(n >= 1, n <= total))
         def _():
@@ -256,41 +274,41 @@
         weight = pltpu.roll(jnp.where(low, second, first), size, 1)
         return (jnp.where(low, first, second) / weight).astype(BF16)
 
+    def block(h, half, r):
+        at = pl.multiple_of((h * 2 + half) * pair, pair)
+        return all_ref.at[pl.ds(r * tp, tp), pl.ds(at, pair)]
+
     def a_copy(r):
         return remote(asend.at[r], abuf.at[y, r], as_.at[r], ar.at[r], at_y)
+
+    def ax_copy(half, r, k):
+        return remote(abuf.at[half, r], xbuf.at[half, r], axs.at[k, r], axr.at[k, r], at_x)
+
+    def ac_copy(src, h, half, r, k):
+        return remote(src.at[half, r], block(h, half, r), acs.at[k, r], acr.at[k, r], at_c)
+
+    def keep(src, h, half, r, k):
+        return pltpu.make_async_copy(src.at[half, r], block(h, half, r), al.at[k, r])
 
     for r in range(TAIL):
         asend[r] = finish(rows + r * tp)
         a_copy(r).start()
     for r in range(TAIL):
         abuf[y, r] = finish(r * tp)
-    for copy in loads[3:]:
-        copy.wait()
-
-    def c_out(r, which):
-        return remote(csend.at[r, which], crecv.at[r, which], ocs.at[r, which], ocr.at[r, which], at_c)
-
-    x_outs = []
+        ax_copy(y, r, 0).start()
+    for r in range(TAIL):
+        ac_copy(abuf, head, y, r, 0).start()
+        keep(abuf, head, y, r, 0).start()
     for r in range(TAIL):
         a_copy(r).wait_recv()
-        feats = jnp.concatenate([abuf[0, r], abuf[1, r]], axis=1)
-        csend[r, 0] = jnp.dot(feats, wo[dhead], preferred_element_type=F32).astype(BF16)
-        c_out(r, 0).start()
-        part[r, 0] = jnp.dot(feats, wo[xhead], preferred_element_type=F32)
-        csend[r, 1] = jnp.dot(feats, wo[chead], preferred_element_type=F32).astype(BF16)
-        c_out(r, 1).start()
-        part[r, 1] = jnp.dot(feats, wo[head], preferred_element_type=F32)
-    for r in range(TAIL):
-        c_out(r, 0).wait_recv()
-        xsend[r] = (part[r, 0] + crecv[r, 0].astype(F32)).astype(BF16)
-        x_out = remote(xsend.at[r], xrecv.at[r], oxs.at[r], oxr.at[r], at_x)
-        x_out.start()
-        x_outs.append(x_out)
-    for r in range(TAIL):
-        c_out(r, 1).wait_recv()
-        x_outs[r].wait_recv()
-        whole = part[r, 1] + crecv[r, 1].astype(F32) + xrecv[r].astype(F32)
-        out_ref[r * tp:(r + 1) * tp, :] = whole.astype(BF16)
+        ax_copy(oy, r, 1).start()
+        ac_copy(abuf, head, oy, r, 1).start()
+        keep(abuf, head, oy, r, 1).start()
+    for k, half in ((0, y), (1, oy)):
+        for r in range(TAIL):
+            ax_copy(half, r, k).wait_recv()
+            ac_copy(xbuf, xhead, half, r, 2 + k).start()
+            keep(xbuf, xhead, half, r, 2 + k).start()
 
     def drain(n, carry):
         origin, s = slot_of(n)
@@ -312,11 +330,16 @@
     lax.fori_loop(0, total, drain, 0)
     for j in range(CHUNKS):
         q_copy(j).wait_send()
-    for j in range(TAIL):
-        c_out(j, 0).wait_send()
-        c_out(j, 1).wait_send()
-        x_outs[j].wait_send()
-        a_copy(j).wait_send()
+    for which in range(3):
+        w_copy(which).wait()
+    w_own().wait()
+    for r in range(TAIL):
+        a_copy(r).wait_send()
+        for k, half in ((0, y), (1, oy)):
+            ax_copy(half, r, k).wait_send()
+            for base, src, h in ((0, abuf, head), (2, xbuf, xhead)):
+                ac_copy(src, h, half, r, base + k).wait()
+                keep(src, h, half, r, base + k).wait()
 
 
 def shards(depth, tokens, gain, w_query, w_key, w_value, w_out, temper, adjacency, order):
@@ -331,17 +354,19 @@
     smem = pl.BlockSpec(memory_space=pltpu.SMEM)
     vmem = pl.BlockSpec(memory_space=pltpu.VMEM)
     hbm = pl.BlockSpec(memory_space=pl.ANY)
-    return pl.pallas_call(
+    attended, weights = pl.pallas_call(
         functools.partial(kernel, depth),
-        out_shape=jax.ShapeDtypeStruct((rows, cols), BF16),
+        out_shape=(
+            jax.ShapeDtypeStruct((rows, count * width), BF16),
+            jax.ShapeDtypeStruct((count * width, cols), BF16),
+        ),
         in_specs=[smem, smem, smem, vmem, hbm, hbm, hbm, hbm, hbm],
-        out_specs=vmem,
+        out_specs=(hbm, hbm),
         scratch_shapes=[
             pltpu.VMEM((total, count, rp, cols), BF16),
             pltpu.VMEM((features, width), BF16),
             pltpu.VMEM((features, width), BF16),
             pltpu.VMEM((features, width), BF16),
-            pltpu.VMEM((count, width, cols), BF16),
             pltpu.VMEM((width, width), BF16),
             pltpu.VMEM((total, 2, 2, rp, pair), BF16),
             pltpu.VMEM((total, 2, rp, pair), BF16),
@@ -351,12 +376,8 @@
             pltpu.VMEM((2, 2 * rows, pair), F32),
             pltpu.VMEM((TAIL, tp, pair), BF16),
             pltpu.VMEM((2, TAIL, tp, pair), BF16),
-            pltpu.VMEM((TAIL, 2, tp, cols), F32),
-            pltpu.VMEM((TAIL, 2, tp, cols), BF16),
-            pltpu.VMEM((TAIL, 2, tp, cols), BF16),
-            pltpu.VMEM((TAIL, tp, cols), BF16),
-            pltpu.VMEM((TAIL, tp, cols), BF16),
-            dma((3 + count,)),
+            pltpu.VMEM((2, TAIL, tp, pair), BF16),
+            dma((3,)),
             dma((CHUNKS,)),
             dma((2, total)),
             dma((total,)),
@@ -370,15 +391,20 @@
             dma((CHUNKS,)),
             dma((TAIL,)),
             dma((TAIL,)),
-            dma((TAIL, 2)),
-            dma((TAIL, 2)),
-            dma((TAIL,)),
-            dma((TAIL,)),
+            dma((2, TAIL)),
+            dma((2, TAIL)),
+            dma((4, TAIL)),
+            dma((4, TAIL)),
+            dma((4, TAIL)),
+            dma((3,)),
+            dma((3,)),
+            dma,
         ],
         compiler_params=pltpu.CompilerParams(
             collective_id=0, has_side_effects=True, vmem_limit_bytes=56 * 1024 * 1024
         ),
     )(order, adjacency, temper, gain.reshape(1, features), tokens, w_query, w_key, w_value, w_out)
+    return jnp.dot(attended, weights, preferred_element_type=F32).astype(BF16)
 
 
 def solution(mesh):

time: 43 us -> 39.6 us (0.921)
  Pallas kernels: 41.2 us -> 37.3 us
  matrix products: 0 us -> 2.16 us
  local copies, waits for them, and re-layouts: 1.57 us -> 0 us
    pallas_call x1, Pallas kernels: 41.2 us -> 37.3 us  [shards(): pl.pallas_call(functools.partial(kernel, depth), out_shape=(jax.ShapeDtyp...]
    dot_general x0 -> x1, matrix products: none -> 2.16 us  [shards(): return jnp.dot(attended, weights, preferred_element_type=F32).astype(BF16)]
    unnamed x1 -> x0, local copies, waits for them, and re-layouts: 1.57 us -> none
where the time goes in v4:
time: 39.6 us; the launch traced here: 39.4 us
  Pallas kernels  37.3 us (94%)
  matrix products  2.16 us (5%)
    pallas_call x1, Pallas kernels, shards(): pl.pallas_call(functools.partial(kernel, depth), out_shape=(jax.ShapeDtyp...  37.3 us
    dot_general x1, matrix products, shards(): return jnp.dot(attended, weights, preferred_element_type=F32).astype(BF16)  2.16 us

profile of v4, /device:TPU:0, one launch (start us, length us, event | category | flops | bytes accessed | tf_op | source)
XLA Modules:
  0.0 39.4 jit_solution(7047829467602626099)
XLA Ops:
  0.0 37.3 %shard_map.91 = (bf16[256,1024]{1,0:T(8,128)(2,1)}, bf16[1024,256]{1,0:T(8,128)(2,1)}) custom-call(s32[16]{0:T(128)} %order_ref.1, s32[16,16]{1,0:T(8,128)} %adj_ref.1, f32[4]{0:T(128)} %temper_ref.1, f32[1,1024]{1,0:T(1,128)} %bitcast.3, bf16[256,256]{1,0:T(8,128)(2,1)} %tokens_ref.1, bf16[1024,256]{1,0:T(8,128)(2,1)} %wq_hbm.1, bf16[1024,256]{1,0:T(8,128)(2,1)} %wk_hbm.1, ...), custom_call_target="tpu_custom_call" | custom-call | tf_op jit(solution)/shard_map/pallas_call | solution.py:357
  37.3 2.2 %convolution_convert_fusion = bf16[256,256]{1,0:T(8,128)(2,1)} fusion(bf16[256,1024]{1,0:T(8,128)(2,1)} %get-tuple-element.7, bf16[1024,256]{1,0:T(8,128)(2,1)} %get-tuple-element.8), kind=kOutput, calls=%fused_computation | convolution fusion | flops 134283264 | bytes 1179648 | tf_op jit(solution)/shard_map/dot_general | solution.py:407

commit v5 on v4

--- a/solution.py
+++ b/solution.py
@@ -48,11 +48,12 @@
     rp = rows // CHUNKS
     total = depth * CHUNKS
     features = wq.shape[0]
-    lag = CHUNKS + 1
+    lag = CHUNKS + 2
     has_left, has_right = line > 0, line < depth - 1
     at_left, at_right = (ctx - 2, head), (ctx + 2, head)
     at_y = (line * 2 + oy, head)
     at_x = (ctx, ox * 2 + c)
+    at_xy = (line * 2 + oy, ox * 2 + c)
     at_c = (ctx, x * 2 + oc)
     xhead = ox * 2 + c
     chead = x * 2 + oc
@@ -78,7 +79,7 @@
         copy.start()
 
     barrier = pltpu.get_barrier_semaphore()
-    for where in (at_y, at_x, at_c, at_d):
+    for where in (at_y, at_x, at_c, at_d, at_xy):
         pl.semaphore_signal(barrier, inc=1, device_id=where, device_id_type=MESH)
 
     @pl.when(has_left)
@@ -93,7 +94,7 @@
     col_id = lax.broadcasted_iota(jnp.int32, (width, width), 1) // size
     mean_mat[...] = jnp.where(row_id == col_id, 1.0 / size, 0.0).astype(BF16)
     acc[...] = jnp.zeros_like(acc)
-    pl.semaphore_wait(barrier, 4 + has_left.astype(jnp.int32) + has_right.astype(jnp.int32))
+    pl.semaphore_wait(barrier, 5 + has_left.astype(jnp.int32) + has_right.astype(jnp.int32))
 
     def slot_of(n):
         origin, j = visit(line, depth, n)
@@ -144,10 +145,13 @@
     for h in range(heads):
         scale = jnp.where(lane_w == h, temper_ref[h] * (LOG2E / size), scale)
 
-    def project(n):
+    def tokens_here(n):
         origin, s = slot_of(n)
         c_copy(s, chead, 0).wait_recv()
         c_copy(s, dhead, 1).wait_recv()
+
+    def project(n):
+        origin, s = slot_of(n)
         parts = [tok[s, h].astype(F32) for h in range(count)]
         squares = parts[0] * parts[0]
         for p in parts[1:]:
@@ -161,8 +165,13 @@
         for half in range(2):
             kvh[s, half, 0] = keys[:, half * pair:(half + 1) * pair]
             kvh[s, half, 1] = values[:, half * pair:(half + 1) * pair]
+        return normed
+
+    def send_pair(n):
+        origin, s = slot_of(n)
         y_copy(s).start()
 
+    def ask(n, normed):
         @pl.when(n < CHUNKS)
         def _():
             query = unit(jnp.dot(normed, wq[...], preferred_element_type=F32))
@@ -189,11 +198,18 @@
     q_blocks = [order_ref[(line * 2 + side) * local + i] for side in (y, oy) for i in range(local)]
     key_lane = lax.broadcasted_iota(jnp.int32, (1, 2 * rp), 1) // BLOCK
 
-    def attend(n):
+    def pair_here(n):
         origin, s = slot_of(n)
         y_copy(s).wait_recv()
+
+    def fetch(n):
+        origin, s = slot_of(n)
         keys = jnp.concatenate([kvh[s, y, 0], kvr[s, 0]], axis=0)
         values = jnp.concatenate([kvh[s, y, 1], kvr[s, 1]], axis=0)
+        return keys, values
+
+    def attend(n, keys, values):
+        origin, s = slot_of(n)
         first = (s - origin * CHUNKS) * per_chunk
         k_blocks = [order_ref[(origin * 2 + side) * local + first + i] for side in (y, oy) for i in range(per_chunk)]
         masks = []
@@ -251,17 +267,30 @@
                 w_copy(which).start()
             w_own().start()
 
-        @pl.when(jnp.logical_and(n >= 1, n <= total))
-        def _():
+        @pl.when(jnp.logical_and(n >= 1, n < lag))
+        def _():
+            tokens_here(n - 1)
+            normed = project(n - 1)
+            send_pair(n - 1)
+            ask(n - 1, normed)
+
+        @pl.when(n == lag)
+        def _():
+            split_queries()
+
+        @pl.when(jnp.logical_and(n >= lag, n <= total))
+        def _():
+            tokens_here(n - 1)
+            pair_here(n - lag)
+            keys, values = fetch(n - lag)
             project(n - 1)
-
-        @pl.when(n == lag)
-        def _():
-            split_queries()
-
-        @pl.when(n >= lag)
-        def _():
-            attend(n - lag)
+            attend(n - lag, keys, values)
+            send_pair(n - 1)
+
+        @pl.when(n > total)
+        def _():
+            pair_here(n - lag)
+            attend(n - lag, *fetch(n - lag))
 
         return carry
 
@@ -281,8 +310,11 @@
     def a_copy(r):
         return remote(asend.at[r], abuf.at[y, r], as_.at[r], ar.at[r], at_y)
 
-    def ax_copy(half, r, k):
-        return remote(abuf.at[half, r], xbuf.at[half, r], axs.at[k, r], axr.at[k, r], at_x)
+    def ax_copy(r):
+        return remote(abuf.at[y, r], xbuf.at[y, r], axs.at[0, r], axr.at[0, r], at_x)
+
+    def axy_copy(r):
+        return remote(asend.at[r], xbuf.at[y, r], axs.at[1, r], axr.at[1, r], at_xy)
 
     def ac_copy(src, h, half, r, k):
         return remote(src.at[half, r], block(h, half, r), acs.at[k, r], acr.at[k, r], at_c)
@@ -292,21 +324,21 @@
 
     for r in range(TAIL):
         asend[r] = finish(rows + r * tp)
+        axy_copy(r).start()
         a_copy(r).start()
     for r in range(TAIL):
         abuf[y, r] = finish(r * tp)
-        ax_copy(y, r, 0).start()
+        ax_copy(r).start()
     for r in range(TAIL):
         ac_copy(abuf, head, y, r, 0).start()
         keep(abuf, head, y, r, 0).start()
     for r in range(TAIL):
         a_copy(r).wait_recv()
-        ax_copy(oy, r, 1).start()
         ac_copy(abuf, head, oy, r, 1).start()
         keep(abuf, head, oy, r, 1).start()
-    for k, half in ((0, y), (1, oy)):
-        for r in range(TAIL):
-            ax_copy(half, r, k).wait_recv()
+    for r in range(TAIL):
+        for k, half, copy in ((1, oy, axy_copy), (0, y, ax_copy)):
+            copy(r).wait_recv()
             ac_copy(xbuf, xhead, half, r, 2 + k).start()
             keep(xbuf, xhead, half, r, 2 + k).start()
 
@@ -335,8 +367,9 @@
     w_own().wait()
     for r in range(TAIL):
         a_copy(r).wait_send()
+        ax_copy(r).wait_send()
+        axy_copy(r).wait_send()
         for k, half in ((0, y), (1, oy)):
-            ax_copy(half, r, k).wait_send()
             for base, src, h in ((0, abuf, head), (2, xbuf, xhead)):
                 ac_copy(src, h, half, r, base + k).wait()
                 keep(src, h, half, r, base + k).wait()

time: 39.6 us -> 37 us (0.934)
  Pallas kernels: 37.3 us -> 34.6 us
    pallas_call x1, Pallas kernels: 37.3 us -> 34.6 us  [shards(): pl.pallas_call(functools.partial(kernel, depth), out_shape=(jax.ShapeDtyp...]
where the time goes in v5:
time: 37 us; the launch traced here: 36.8 us
  Pallas kernels  34.6 us (94%)
  matrix products  2.16 us (6%)
    pallas_call x1, Pallas kernels, shards(): pl.pallas_call(functools.partial(kernel, depth), out_shape=(jax.ShapeDtyp...  34.6 us
    dot_general x1, matrix products, shards(): return jnp.dot(attended, weights, preferred_element_type=F32).astype(BF16)  2.16 us

profile of v5, /device:TPU:0, one launch (start us, length us, event | category | flops | bytes accessed | tf_op | source)
XLA Modules:
  0.0 36.8 jit_solution(12781053219628692359)
XLA Ops:
  0.0 34.6 %shard_map.91 = (bf16[256,1024]{1,0:T(8,128)(2,1)}, bf16[1024,256]{1,0:T(8,128)(2,1)}) custom-call(s32[16]{0:T(128)} %order_ref.1, s32[16,16]{1,0:T(8,128)} %adj_ref.1, f32[4]{0:T(128)} %temper_ref.1, f32[1,1024]{1,0:T(1,128)} %bitcast.3, bf16[256,256]{1,0:T(8,128)(2,1)} %tokens_ref.1, bf16[1024,256]{1,0:T(8,128)(2,1)} %wq_hbm.1, bf16[1024,256]{1,0:T(8,128)(2,1)} %wk_hbm.1, ...), custom_call_target="tpu_custom_call" | custom-call | tf_op jit(solution)/shard_map/pallas_call | solution.py:390
  34.6 2.2 %convolution_convert_fusion = bf16[256,256]{1,0:T(8,128)(2,1)} fusion(bf16[256,1024]{1,0:T(8,128)(2,1)} %get-tuple-element.7, bf16[1024,256]{1,0:T(8,128)(2,1)} %get-tuple-element.8), kind=kOutput, calls=%fused_computation | convolution fusion | flops 134283264 | bytes 1179648 | tf_op jit(solution)/shard_map/dot_general | solution.py:440

commit v6 on v5

--- a/solution.py
+++ b/solution.py
@@ -208,7 +208,7 @@
         values = jnp.concatenate([kvh[s, y, 1], kvr[s, 1]], axis=0)
         return keys, values
 
-    def attend(n, keys, values):
+    def attend(n, keys, values, sides):
         origin, s = slot_of(n)
         first = (s - origin * CHUNKS) * per_chunk
         k_blocks = [order_ref[(origin * 2 + side) * local + first + i] for side in (y, oy) for i in range(per_chunk)]
@@ -219,13 +219,18 @@
                 mask = jnp.where(key_lane == i, (adj_ref[qb, kb] > 0).astype(F32), mask)
             masks.append(mask)
         ones = jnp.ones_like(values)
+        at, to = sides[0] * rows, (sides[-1] + 1) * rows
         for h in range(2):
             mine = jnp.where(low, values, ones) if h == 0 else jnp.where(low, ones, values)
-            scores = lax.dot_general(qm[h], keys, (((1,), (1,)), ((), ())), preferred_element_type=F32)
+            scores = lax.dot_general(qm[h, at:to, :], keys, (((1,), (1,)), ((), ())), preferred_element_type=F32)
             probs = jnp.concatenate(
-                [(jnp.exp2(scores[i * BLOCK:(i + 1) * BLOCK]) * masks[i]).astype(BF16) for i in range(2 * local)], axis=0
+                [
+                    (jnp.exp2(scores[i * BLOCK:(i + 1) * BLOCK]) * masks[at // BLOCK + i]).astype(BF16)
+                    for i in range((to - at) // BLOCK)
+                ],
+                axis=0,
             )
-            acc[h] += jnp.dot(probs, mine, preferred_element_type=F32)
+            acc[h, at:to, :] += jnp.dot(probs, mine, preferred_element_type=F32)
 
     def w_columns(h):
         return wo_hbm.at[:, pl.ds(pl.multiple_of(h * cols, cols), cols)]
@@ -267,7 +272,7 @@
                 w_copy(which).start()
             w_own().start()
 
-        @pl.when(jnp.logical_and(n >= 1, n < lag))
+        @pl.when(jnp.logical_or(jnp.logical_and(n >= 1, n < lag), n == total))
         def _():
             tokens_here(n - 1)
             normed = project(n - 1)
@@ -278,23 +283,23 @@
         def _():
             split_queries()
 
-        @pl.when(jnp.logical_and(n >= lag, n <= total))
+        @pl.when(jnp.logical_and(n >= lag, n < total))
         def _():
             tokens_here(n - 1)
             pair_here(n - lag)
             keys, values = fetch(n - lag)
             project(n - 1)
-            attend(n - lag, keys, values)
+            attend(n - lag, keys, values, (0, 1))
             send_pair(n - 1)
 
-        @pl.when(n > total)
+        @pl.when(n >= total)
         def _():
             pair_here(n - lag)
-            attend(n - lag, *fetch(n - lag))
+            attend(n - lag, *fetch(n - lag), (0, 1))
 
         return carry
 
-    lax.fori_loop(0, total + lag, step, 0)
+    lax.fori_loop(0, total + lag - 1, step, 0)
 
     tp = rows // TAIL
 
@@ -322,25 +327,20 @@
     def keep(src, h, half, r, k):
         return pltpu.make_async_copy(src.at[half, r], block(h, half, r), al.at[k, r])
 
+    pair_here(total - 1)
+    keys, values = fetch(total - 1)
+    attend(total - 1, keys, values, (1,))
     for r in range(TAIL):
         asend[r] = finish(rows + r * tp)
         axy_copy(r).start()
         a_copy(r).start()
+    attend(total - 1, keys, values, (0,))
     for r in range(TAIL):
         abuf[y, r] = finish(r * tp)
         ax_copy(r).start()
     for r in range(TAIL):
         ac_copy(abuf, head, y, r, 0).start()
         keep(abuf, head, y, r, 0).start()
-    for r in range(TAIL):
-        a_copy(r).wait_recv()
-        ac_copy(abuf, head, oy, r, 1).start()
-        keep(abuf, head, oy, r, 1).start()
-    for r in range(TAIL):
-        for k, half, copy in ((1, oy, axy_copy), (0, y, ax_copy)):
-            copy(r).wait_recv()
-            ac_copy(xbuf, xhead, half, r, 2 + k).start()
-            keep(xbuf, xhead, half, r, 2 + k).start()
 
     def drain(n, carry):
         origin, s = slot_of(n)
@@ -362,6 +362,16 @@
     lax.fori_loop(0, total, drain, 0)
     for j in range(CHUNKS):
         q_copy(j).wait_send()
+    for r in range(TAIL):
+        a_copy(r).wait_recv()
+        ac_copy(abuf, head, oy, r, 1).start()
+        keep(abuf, head, oy, r, 1).start()
+    for r in range(TAIL):
+        for k, half, copy in ((1, oy, axy_copy), (0, y, ax_copy)):
+            copy(r).wait_recv()
+            ac_copy(xbuf, xhead, half, r, 2 + k).start()
+            keep(xbuf, xhead, half, r, 2 + k).start()
+
     for which in range(3):
         w_copy(which).wait()
     w_own().wait()

time: 37 us -> 36.9 us (level)
  no operation moved by 1% of the time
where the time goes in v6:
time: 36.9 us; the launch traced here: 36.7 us
  Pallas kernels  34.5 us (93%)
  matrix products  2.16 us (6%)
    pallas_call x1, Pallas kernels, shards(): pl.pallas_call(functools.partial(kernel, depth), out_shape=(jax.ShapeDtyp...  34.5 us
    dot_general x1, matrix products, shards(): return jnp.dot(attended, weights, preferred_element_type=F32).astype(BF16)  2.16 us

profile of v6, /device:TPU:0, one launch (start us, length us, event | category | flops | bytes accessed | tf_op | source)
XLA Modules:
  0.0 36.7 jit_solution(18375960173829071732)
XLA Ops:
  0.0 34.5 %shard_map.91 = (bf16[256,1024]{1,0:T(8,128)(2,1)}, bf16[1024,256]{1,0:T(8,128)(2,1)}) custom-call(s32[16]{0:T(128)} %order_ref.1, s32[16,16]{1,0:T(8,128)} %adj_ref.1, f32[4]{0:T(128)} %temper_ref.1, f32[1,1024]{1,0:T(1,128)} %bitcast.3, bf16[256,256]{1,0:T(8,128)(2,1)} %tokens_ref.1, bf16[1024,256]{1,0:T(8,128)(2,1)} %wq_hbm.1, bf16[1024,256]{1,0:T(8,128)(2,1)} %wk_hbm.1, ...), custom_call_target="tpu_custom_call" | custom-call | tf_op jit(solution)/shard_map/pallas_call | solution.py:400
  34.5 2.2 %convolution_convert_fusion = bf16[256,256]{1,0:T(8,128)(2,1)} fusion(bf16[256,1024]{1,0:T(8,128)(2,1)} %get-tuple-element.7, bf16[1024,256]{1,0:T(8,128)(2,1)} %get-tuple-element.8), kind=kOutput, calls=%fused_computation | convolution fusion | flops 134283264 | bytes 1179648 | tf_op jit(solution)/shard_map/dot_general | solution.py:450

commit v7 on v6

--- a/solution.py
+++ b/solution.py
@@ -29,12 +29,16 @@
     return origin, jnp.where(n < CHUNKS, n, t % CHUNKS)
 
 
+def group_of(depth):
+    return 4 if depth % 4 == 0 else 2 if depth % 2 == 0 else 1
+
+
 def kernel(
     depth,
     order_ref, adj_ref, temper_ref, gain_ref, tokens_ref, wq_hbm, wk_hbm, wv_hbm, wo_hbm,
     all_ref, wall_ref,
     tok, wq, wk, wv, mean_mat, kvh, kvr, qh, qr, qm, acc, asend, abuf, xbuf,
-    w_sem, t_sem, zs, zr, xs, xr, cs, cr, ys, yr, qs, qrs, as_, ar, axs, axr, acs, acr, al, ws, wr, wl,
+    w_sem, t_sem, zs, zr, xs, xr, cs, cr, ys, yr, qs, qrs, as_, ar, axs, axr, acs, acr, al, ws, wr, wl, wzs, wzr,
 ):
     ctx, head = lax.axis_index("ctx"), lax.axis_index("head")
     line, y = ctx // 2, ctx % 2
@@ -59,6 +63,13 @@
     chead = x * 2 + oc
     dhead = ox * 2 + oc
     at_d = (ctx, dhead)
+    group = group_of(depth)
+    base, place = line // group * group, line % group
+    share = width // group
+
+    def peer(d):
+        return ((base + (place + d) % group) * 2 + y, head)
+
 
     def remote(src, dst, send, recv, where):
         return pltpu.make_async_remote_copy(
@@ -79,7 +90,7 @@
         copy.start()
 
     barrier = pltpu.get_barrier_semaphore()
-    for where in (at_y, at_x, at_c, at_d, at_xy):
+    for where in [at_y, at_x, at_c, at_d, at_xy] + [peer(d) for d in range(1, group)]:
         pl.semaphore_signal(barrier, inc=1, device_id=where, device_id_type=MESH)
 
     @pl.when(has_left)
@@ -94,7 +105,7 @@
     col_id = lax.broadcasted_iota(jnp.int32, (width, width), 1) // size
     mean_mat[...] = jnp.where(row_id == col_id, 1.0 / size, 0.0).astype(BF16)
     acc[...] = jnp.zeros_like(acc)
-    pl.semaphore_wait(barrier, 5 + has_left.astype(jnp.int32) + has_right.astype(jnp.int32))
+    pl.semaphore_wait(barrier, 4 + group + has_left.astype(jnp.int32) + has_right.astype(jnp.int32))
 
     def slot_of(n):
         origin, j = visit(line, depth, n)
@@ -238,9 +249,23 @@
     def w_rows(h):
         return wall_ref.at[pl.ds(pl.multiple_of(h * width, width), width), :]
 
+    def w_piece(h, part):
+        return wall_ref.at[pl.ds(pl.multiple_of(h * width + part * share, share), share), :]
+
     def w_copy(which):
-        h, where = ((xhead, at_x), (dhead, at_d), (chead, at_c))[which]
-        return remote(w_columns(h), w_rows(head), ws.at[which], wr.at[which], where)
+        h, where = ((xhead, at_x), (dhead, at_d))[which]
+        source = wo_hbm.at[
+            pl.ds(pl.multiple_of(place * share, share), share), pl.ds(pl.multiple_of(h * cols, cols), cols)
+        ]
+        return remote(source, w_piece(head, place), ws.at[which], wr.at[which], where)
+
+    def w_core():
+        return remote(w_columns(chead), w_rows(head), ws.at[2], wr.at[2], at_c)
+
+    def w_along(d, which):
+        h = (xhead, dhead)[which]
+        piece = w_piece(h, place)
+        return remote(piece, piece, wzs.at[d - 1, which], wzr.at[d - 1, which], peer(d))
 
     def w_own():
         return pltpu.make_async_copy(w_columns(head), w_rows(head), wl)
@@ -266,11 +291,19 @@
             x_copy(s, xhead).wait_recv()
             c_copy(s, xhead, 1).start()
 
-        @pl.when(n == total - 1)
-        def _():
-            for which in range(3):
-                w_copy(which).start()
+        @pl.when(n == 1)
+        def _():
+            w_copy(0).start()
+            w_copy(1).start()
+            w_core().start()
             w_own().start()
+
+        @pl.when(n == total - 2)
+        def _():
+            for which in range(2):
+                w_copy(which).wait_recv()
+                for d in range(1, group):
+                    w_along(d, which).start()
 
         @pl.when(jnp.logical_or(jnp.logical_and(n >= 1, n < lag), n == total))
         def _():
@@ -372,8 +405,11 @@
             ac_copy(xbuf, xhead, half, r, 2 + k).start()
             keep(xbuf, xhead, half, r, 2 + k).start()
 
-    for which in range(3):
-        w_copy(which).wait()
+    for which in range(2):
+        w_copy(which).wait_send()
+        for d in range(1, group):
+            w_along(d, which).wait()
+    w_core().wait()
     w_own().wait()
     for r in range(TAIL):
         a_copy(r).wait_send()
@@ -442,6 +478,8 @@
             dma((3,)),
             dma((3,)),
             dma,
+            dma((max(group_of(depth) - 1, 1), 2)),
+            dma((max(group_of(depth) - 1, 1), 2)),
         ],
         compiler_params=pltpu.CompilerParams(
             collective_id=0, has_side_effects=True, vmem_limit_bytes=56 * 1024 * 1024

time: 36.9 us -> 38.5 us (1.043)
  Pallas kernels: 34.5 us -> 36.1 us
    pallas_call x1, Pallas kernels: 34.5 us -> 36.1 us  [shards(): pl.pallas_call(functools.partial(kernel, depth), out_shape=(jax.ShapeDtyp...]
where the time goes in v7:
time: 38.5 us; the launch traced here: 38.3 us
  Pallas kernels  36.1 us (94%)
  matrix products  2.16 us (6%)
    pallas_call x1, Pallas kernels, shards(): pl.pallas_call(functools.partial(kernel, depth), out_shape=(jax.ShapeDtyp...  36.1 us
    dot_general x1, matrix products, shards(): return jnp.dot(attended, weights, preferred_element_type=F32).astype(BF16)  2.16 us

profile of v7, /device:TPU:0, one launch (start us, length us, event | category | flops | bytes accessed | tf_op | source)
XLA Modules:
  0.0 38.3 jit_solution(9462472200657744025)
XLA Ops:
  0.0 36.1 %shard_map.91 = (bf16[256,1024]{1,0:T(8,128)(2,1)}, bf16[1024,256]{1,0:T(8,128)(2,1)}) custom-call(s32[16]{0:T(128)} %order_ref.1, s32[16,16]{1,0:T(8,128)} %adj_ref.1, f32[4]{0:T(128)} %temper_ref.1, f32[1,1024]{1,0:T(1,128)} %bitcast.3, bf16[256,256]{1,0:T(8,128)(2,1)} %tokens_ref.1, bf16[1024,256]{1,0:T(8,128)(2,1)} %wq_hbm.1, bf16[1024,256]{1,0:T(8,128)(2,1)} %wk_hbm.1, ...), custom_call_target="tpu_custom_call" | custom-call | tf_op jit(solution)/shard_map/pallas_call | solution.py:436
  36.1 2.2 %convolution_convert_fusion = bf16[256,256]{1,0:T(8,128)(2,1)} fusion(bf16[256,1024]{1,0:T(8,128)(2,1)} %get-tuple-element.7, bf16[1024,256]{1,0:T(8,128)(2,1)} %get-tuple-element.8), kind=kOutput, calls=%fused_computation | convolution fusion | flops 134283264 | bytes 1179648 | tf_op jit(solution)/shard_map/dot_general | solution.py:488

commit v8 on v6

--- a/solution.py
+++ b/solution.py
@@ -34,7 +34,7 @@
     order_ref, adj_ref, temper_ref, gain_ref, tokens_ref, wq_hbm, wk_hbm, wv_hbm, wo_hbm,
     all_ref, wall_ref,
     tok, wq, wk, wv, mean_mat, kvh, kvr, qh, qr, qm, acc, asend, abuf, xbuf,
-    w_sem, t_sem, zs, zr, xs, xr, cs, cr, ys, yr, qs, qrs, as_, ar, axs, axr, acs, acr, al, ws, wr, wl,
+    w_sem, t_sem, zs, zes, zr, xs, xr, cs, cr, ys, yr, qs, qrs, as_, ar, axs, axr, acs, acr, al, ws, wr, wl,
 ):
     ctx, head = lax.axis_index("ctx"), lax.axis_index("head")
     line, y = ctx // 2, ctx % 2
@@ -59,6 +59,11 @@
     chead = x * 2 + oc
     dhead = ox * 2 + oc
     at_d = (ctx, dhead)
+    is_end = jnp.logical_or(line == 0, line == depth - 1)
+
+    def on_line(d):
+        return ((line + d) % depth * 2 + y, head)
+
 
     def remote(src, dst, send, recv, where):
         return pltpu.make_async_remote_copy(
@@ -79,22 +84,14 @@
         copy.start()
 
     barrier = pltpu.get_barrier_semaphore()
-    for where in (at_y, at_x, at_c, at_d, at_xy):
+    for where in [at_y, at_x, at_c, at_d, at_xy] + [on_line(d) for d in range(1, depth)]:
         pl.semaphore_signal(barrier, inc=1, device_id=where, device_id_type=MESH)
-
-    @pl.when(has_left)
-    def _():
-        pl.semaphore_signal(barrier, inc=1, device_id=at_left, device_id_type=MESH)
-
-    @pl.when(has_right)
-    def _():
-        pl.semaphore_signal(barrier, inc=1, device_id=at_right, device_id_type=MESH)
 
     row_id = lax.broadcasted_iota(jnp.int32, (width, width), 0) // size
     col_id = lax.broadcasted_iota(jnp.int32, (width, width), 1) // size
     mean_mat[...] = jnp.where(row_id == col_id, 1.0 / size, 0.0).astype(BF16)
     acc[...] = jnp.zeros_like(acc)
-    pl.semaphore_wait(barrier, 5 + has_left.astype(jnp.int32) + has_right.astype(jnp.int32))
+    pl.semaphore_wait(barrier, 4 + depth)
 
     def slot_of(n):
         origin, j = visit(line, depth, n)
@@ -118,21 +115,43 @@
     def q_copy(j):
         return remote(qh.at[oy, j], qr.at[j], qs.at[j], qrs.at[j], at_y)
 
+    def end_copy(d, j):
+        away = jnp.where(line == 0, d, depth - d)
+        s = line * CHUNKS + j
+        return remote(tok.at[s, head], tok.at[s, head], zes.at[d - 1, j], zr.at[s], on_line(away))
+
+    def passes(origin):
+        inner = jnp.logical_and(origin > 0, origin < depth - 1)
+        right = jnp.logical_and(inner, jnp.logical_and(has_right, origin <= line))
+        left = jnp.logical_and(inner, jnp.logical_and(has_left, origin >= line))
+        return left, right
+
     def spread(origin, s):
-        @pl.when(jnp.logical_and(has_right, origin <= line))
+        left, right = passes(origin)
+
+        @pl.when(right)
         def _():
             z_right(s).start()
 
-        @pl.when(jnp.logical_and(has_left, origin >= line))
+        @pl.when(left)
         def _():
             z_left(s).start()
 
         x_copy(s, head).start()
         c_copy(s, head, 0).start()
+
+    first_far = sorted({1, depth - 1} - {0})
+    later_far = [d for d in range(2, depth - 1)]
 
     for j in range(CHUNKS):
         own[j].wait()
         spread(line, line * CHUNKS + j)
+
+        @pl.when(is_end)
+        def _():
+            for d in first_far:
+                end_copy(d, j).start()
+
     for copy in loads:
         copy.wait()
 
@@ -248,6 +267,12 @@
     def step(n, carry):
         away = n // CHUNKS + 1
 
+        @pl.when(jnp.logical_and(is_end, n == 1))
+        def _():
+            for d in later_far:
+                for j in range(CHUNKS):
+                    end_copy(d, j).start()
+
         @pl.when(line - away >= 0)
         def _():
             s = (line - away) * CHUNKS + n % CHUNKS
@@ -345,11 +370,13 @@
     def drain(n, carry):
         origin, s = slot_of(n)
 
-        @pl.when(jnp.logical_and(has_right, origin <= line))
+        left, right = passes(origin)
+
+        @pl.when(right)
         def _():
             z_right(s).wait_send()
 
-        @pl.when(jnp.logical_and(has_left, origin >= line))
+        @pl.when(left)
         def _():
             z_left(s).wait_send()
 
@@ -360,6 +387,13 @@
         return carry
 
     lax.fori_loop(0, total, drain, 0)
+
+    @pl.when(is_end)
+    def _():
+        for d in range(1, depth):
+            for j in range(CHUNKS):
+                end_copy(d, j).wait_send()
+
     for j in range(CHUNKS):
         q_copy(j).wait_send()
     for r in range(TAIL):
@@ -423,6 +457,7 @@
             dma((3,)),
             dma((CHUNKS,)),
             dma((2, total)),
+            dma((max(depth - 1, 1), CHUNKS)),
             dma((total,)),
             dma((total,)),
             dma((total,)),

time: 36.9 us -> 39.9 us (1.081)
  Pallas kernels: 34.5 us -> 37.5 us
    pallas_call x1, Pallas kernels: 34.5 us -> 37.5 us  [shards(): pl.pallas_call(functools.partial(kernel, depth), out_shape=(jax.ShapeDtyp...]
where the time goes in v8:
time: 39.9 us; the launch traced here: 39.7 us
  Pallas kernels  37.5 us (94%)
  matrix products  2.16 us (5%)
    pallas_call x1, Pallas kernels, shards(): pl.pallas_call(functools.partial(kernel, depth), out_shape=(jax.ShapeDtyp...  37.5 us
    dot_general x1, matrix products, shards(): return jnp.dot(attended, weights, preferred_element_type=F32).astype(BF16)  2.16 us

profile of v8, /device:TPU:0, one launch (start us, length us, event | category | flops | bytes accessed | tf_op | source)
XLA Modules:
  0.0 39.7 jit_solution(18074054287030312941)
XLA Ops:
  0.0 37.5 %shard_map.91 = (bf16[256,1024]{1,0:T(8,128)(2,1)}, bf16[1024,256]{1,0:T(8,128)(2,1)}) custom-call(s32[16]{0:T(128)} %order_ref.1, s32[16,16]{1,0:T(8,128)} %adj_ref.1, f32[4]{0:T(128)} %temper_ref.1, f32[1,1024]{1,0:T(1,128)} %bitcast.3, bf16[256,256]{1,0:T(8,128)(2,1)} %tokens_ref.1, bf16[1024,256]{1,0:T(8,128)(2,1)} %wq_hbm.1, bf16[1024,256]{1,0:T(8,128)(2,1)} %wk_hbm.1, ...), custom_call_target="tpu_custom_call" | custom-call | tf_op jit(solution)/shard_map/pallas_call | solution.py:434
  37.5 2.2 %convolution_convert_fusion = bf16[256,256]{1,0:T(8,128)(2,1)} fusion(bf16[256,1024]{1,0:T(8,128)(2,1)} %get-tuple-element.7, bf16[1024,256]{1,0:T(8,128)(2,1)} %get-tuple-element.8), kind=kOutput, calls=%fused_computation | convolution fusion | flops 134283264 | bytes 1179648 | tf_op jit(solution)/shard_map/dot_general | solution.py:485

commit v9 on v6

--- a/solution.py
+++ b/solution.py
@@ -75,9 +75,6 @@
         pltpu.make_async_copy(tokens_ref.at[pl.ds(j * rp, rp), :], tok.at[line * CHUNKS + j, head], t_sem.at[j])
         for j in range(CHUNKS)
     ]
-    for copy in own + loads:
-        copy.start()
-
     barrier = pltpu.get_barrier_semaphore()
     for where in (at_y, at_x, at_c, at_d, at_xy):
         pl.semaphore_signal(barrier, inc=1, device_id=where, device_id_type=MESH)
@@ -90,49 +87,53 @@
     def _():
         pl.semaphore_signal(barrier, inc=1, device_id=at_right, device_id_type=MESH)
 
+    for copy in own:
+        copy.start()
+    pl.semaphore_wait(barrier, 5 + has_left.astype(jnp.int32) + has_right.astype(jnp.int32))
+
+    def slot_of(n):
+        origin, j = visit(line, depth, n)
+        return origin, origin * CHUNKS + j
+
+    def z_right(s):
+        return remote(tok.at[s, head], tok.at[s, head], zs.at[1, s], zr.at[s], at_right)
+
+    def z_left(s):
+        return remote(tok.at[s, head], tok.at[s, head], zs.at[0, s], zr.at[s], at_left)
+
+    def x_copy(s, h):
+        return remote(tok.at[s, h], tok.at[s, h], xs.at[s], xr.at[s], at_x)
+
+    def c_copy(s, h, which):
+        return remote(tok.at[s, h], tok.at[s, h], cs.at[s, which], cr.at[s, which], at_c)
+
+    def y_copy(s):
+        return remote(kvh.at[s, oy], kvr.at[s], ys.at[s], yr.at[s], at_y)
+
+    def q_copy(j):
+        return remote(qh.at[oy, j], qr.at[j], qs.at[j], qrs.at[j], at_y)
+
+    def spread(origin, s):
+        @pl.when(jnp.logical_and(has_right, origin <= line))
+        def _():
+            z_right(s).start()
+
+        @pl.when(jnp.logical_and(has_left, origin >= line))
+        def _():
+            z_left(s).start()
+
+        x_copy(s, head).start()
+        c_copy(s, head, 0).start()
+
+    for j in range(CHUNKS):
+        own[j].wait()
+        spread(line, line * CHUNKS + j)
+    for copy in loads:
+        copy.start()
     row_id = lax.broadcasted_iota(jnp.int32, (width, width), 0) // size
     col_id = lax.broadcasted_iota(jnp.int32, (width, width), 1) // size
     mean_mat[...] = jnp.where(row_id == col_id, 1.0 / size, 0.0).astype(BF16)
     acc[...] = jnp.zeros_like(acc)
-    pl.semaphore_wait(barrier, 5 + has_left.astype(jnp.int32) + has_right.astype(jnp.int32))
-
-    def slot_of(n):
-        origin, j = visit(line, depth, n)
-        return origin, origin * CHUNKS + j
-
-    def z_right(s):
-        return remote(tok.at[s, head], tok.at[s, head], zs.at[1, s], zr.at[s], at_right)
-
-    def z_left(s):
-        return remote(tok.at[s, head], tok.at[s, head], zs.at[0, s], zr.at[s], at_left)
-
-    def x_copy(s, h):
-        return remote(tok.at[s, h], tok.at[s, h], xs.at[s], xr.at[s], at_x)
-
-    def c_copy(s, h, which):
-        return remote(tok.at[s, h], tok.at[s, h], cs.at[s, which], cr.at[s, which], at_c)
-
-    def y_copy(s):
-        return remote(kvh.at[s, oy], kvr.at[s], ys.at[s], yr.at[s], at_y)
-
-    def q_copy(j):
-        return remote(qh.at[oy, j], qr.at[j], qs.at[j], qrs.at[j], at_y)
-
-    def spread(origin, s):
-        @pl.when(jnp.logical_and(has_right, origin <= line))
-        def _():
-            z_right(s).start()
-
-        @pl.when(jnp.logical_and(has_left, origin >= line))
-        def _():
-            z_left(s).start()
-
-        x_copy(s, head).start()
-        c_copy(s, head, 0).start()
-
-    for j in range(CHUNKS):
-        own[j].wait()
-        spread(line, line * CHUNKS + j)
     for copy in loads:
         copy.wait()
 
@@ -246,6 +247,12 @@
         return pltpu.make_async_copy(w_columns(head), w_rows(head), wl)
 
     def step(n, carry):
+        @pl.when(n == jnp.where(line == 0, total - 2 * CHUNKS, total - 1))
+        def _():
+            for which in range(3):
+                w_copy(which).start()
+            w_own().start()
+
         away = n // CHUNKS + 1
 
         @pl.when(line - away >= 0)
@@ -265,12 +272,6 @@
             origin, s = slot_of(n)
             x_copy(s, xhead).wait_recv()
             c_copy(s, xhead, 1).start()
-
-        @pl.when(n == total - 1)
-        def _():
-            for which in range(3):
-                w_copy(which).start()
-            w_own().start()
 
         @pl.when(jnp.logical_or(jnp.logical_and(n >= 1, n < lag), n == total))
         def _():

time: 36.9 us -> 41.3 us (1.12)
  Pallas kernels: 34.5 us -> 39 us
    pallas_call x1, Pallas kernels: 34.5 us -> 39 us  [shards(): pl.pallas_call(functools.partial(kernel, depth), out_shape=(jax.ShapeDtyp...]
where the time goes in v9:
time: 41.3 us; the launch traced here: 41.1 us
  Pallas kernels  39 us (94%)
  matrix products  2.16 us (5%)
    pallas_call x1, Pallas kernels, shards(): pl.pallas_call(functools.partial(kernel, depth), out_shape=(jax.ShapeDtyp...  39 us
    dot_general x1, matrix products, shards(): return jnp.dot(attended, weights, preferred_element_type=F32).astype(BF16)  2.16 us

profile of v9, /device:TPU:0, one launch (start us, length us, event | category | flops | bytes accessed | tf_op | source)
XLA Modules:
  0.0 41.1 jit_solution(1887305016525219516)
XLA Ops:
  0.0 39.0 %shard_map.91 = (bf16[256,1024]{1,0:T(8,128)(2,1)}, bf16[1024,256]{1,0:T(8,128)(2,1)}) custom-call(s32[16]{0:T(128)} %order_ref.1, s32[16,16]{1,0:T(8,128)} %adj_ref.1, f32[4]{0:T(128)} %temper_ref.1, f32[1,1024]{1,0:T(1,128)} %bitcast.3, bf16[256,256]{1,0:T(8,128)(2,1)} %tokens_ref.1, bf16[1024,256]{1,0:T(8,128)(2,1)} %wq_hbm.1, bf16[1024,256]{1,0:T(8,128)(2,1)} %wk_hbm.1, ...), custom_call_target="tpu_custom_call" | custom-call | tf_op jit(solution)/shard_map/pallas_call | solution.py:401
  39.0 2.2 %convolution_convert_fusion = bf16[256,256]{1,0:T(8,128)(2,1)} fusion(bf16[256,1024]{1,0:T(8,128)(2,1)} %get-tuple-element.7, bf16[1024,256]{1,0:T(8,128)(2,1)} %get-tuple-element.8), kind=kOutput, calls=%fused_computation | convolution fusion | flops 134283264 | bytes 1179648 | tf_op jit(solution)/shard_map/dot_general | solution.py:451

commit v10 on v7

--- a/solution.py
+++ b/solution.py
@@ -90,7 +90,7 @@
         copy.start()
 
     barrier = pltpu.get_barrier_semaphore()
-    for where in [at_y, at_x, at_c, at_d, at_xy] + [peer(d) for d in range(1, group)]:
+    for where in (at_y, at_x, at_c, at_d, at_xy):
         pl.semaphore_signal(barrier, inc=1, device_id=where, device_id_type=MESH)
 
     @pl.when(has_left)
@@ -105,7 +105,7 @@
     col_id = lax.broadcasted_iota(jnp.int32, (width, width), 1) // size
     mean_mat[...] = jnp.where(row_id == col_id, 1.0 / size, 0.0).astype(BF16)
     acc[...] = jnp.zeros_like(acc)
-    pl.semaphore_wait(barrier, 4 + group + has_left.astype(jnp.int32) + has_right.astype(jnp.int32))
+    pl.semaphore_wait(barrier, 5 + has_left.astype(jnp.int32) + has_right.astype(jnp.int32))
 
     def slot_of(n):
         origin, j = visit(line, depth, n)

time: 38.5 us -> 36.9 us (0.958)
  Pallas kernels: 36.1 us -> 34.6 us
    pallas_call x1, Pallas kernels: 36.1 us -> 34.6 us  [shards(): pl.pallas_call(functools.partial(kernel, depth), out_shape=(jax.ShapeDtyp...]
where the time goes in v10:
time: 36.9 us; the launch traced here: 36.7 us
  Pallas kernels  34.6 us (94%)
  matrix products  2.16 us (6%)
    pallas_call x1, Pallas kernels, shards(): pl.pallas_call(functools.partial(kernel, depth), out_shape=(jax.ShapeDtyp...  34.6 us
    dot_general x1, matrix products, shards(): return jnp.dot(attended, weights, preferred_element_type=F32).astype(BF16)  2.16 us

profile of v10, /device:TPU:0, one launch (start us, length us, event | category | flops | bytes accessed | tf_op | source)
XLA Modules:
  0.0 36.7 jit_solution(13419402418254962354)
XLA Ops:
  0.0 34.6 %shard_map.91 = (bf16[256,1024]{1,0:T(8,128)(2,1)}, bf16[1024,256]{1,0:T(8,128)(2,1)}) custom-call(s32[16]{0:T(128)} %order_ref.1, s32[16,16]{1,0:T(8,128)} %adj_ref.1, f32[4]{0:T(128)} %temper_ref.1, f32[1,1024]{1,0:T(1,128)} %bitcast.3, bf16[256,256]{1,0:T(8,128)(2,1)} %tokens_ref.1, bf16[1024,256]{1,0:T(8,128)(2,1)} %wq_hbm.1, bf16[1024,256]{1,0:T(8,128)(2,1)} %wk_hbm.1, ...), custom_call_target="tpu_custom_call" | custom-call | tf_op jit(solution)/shard_map/pallas_call | solution.py:436
  34.6 2.2 %convolution_convert_fusion = bf16[256,256]{1,0:T(8,128)(2,1)} fusion(bf16[256,1024]{1,0:T(8,128)(2,1)} %get-tuple-element.7, bf16[1024,256]{1,0:T(8,128)(2,1)} %get-tuple-element.8), kind=kOutput, calls=%fused_computation | convolution fusion | flops 134283264 | bytes 1179648 | tf_op jit(solution)/shard_map/dot_general | solution.py:488

commit v11 on v10

--- a/solution.py
+++ b/solution.py
@@ -291,19 +291,10 @@
             x_copy(s, xhead).wait_recv()
             c_copy(s, xhead, 1).start()
 
-        @pl.when(n == 1)
+        @pl.when(n == total - 2)
         def _():
             w_copy(0).start()
             w_copy(1).start()
-            w_core().start()
-            w_own().start()
-
-        @pl.when(n == total - 2)
-        def _():
-            for which in range(2):
-                w_copy(which).wait_recv()
-                for d in range(1, group):
-                    w_along(d, which).start()
 
         @pl.when(jnp.logical_or(jnp.logical_and(n >= 1, n < lag), n == total))
         def _():
@@ -324,6 +315,15 @@
             project(n - 1)
             attend(n - lag, keys, values, (0, 1))
             send_pair(n - 1)
+
+        @pl.when(n == total)
+        def _():
+            w_core().start()
+            w_own().start()
+            for which in range(2):
+                w_copy(which).wait_recv()
+                for d in range(1, group):
+                    w_along(d, which).start()
 
         @pl.when(n >= total)
         def _():

time: 36.9 us -> 37.4 us (1.014)
  Pallas kernels: 34.6 us -> 35 us
    pallas_call x1, Pallas kernels: 34.6 us -> 35 us  [shards(): pl.pallas_call(functools.partial(kernel, depth), out_shape=(jax.ShapeDtyp...]
where the time goes in v11:
time: 37.4 us; the launch traced here: 37.2 us
  Pallas kernels  35 us (94%)
  matrix products  2.16 us (6%)
    pallas_call x1, Pallas kernels, shards(): pl.pallas_call(functools.partial(kernel, depth), out_shape=(jax.ShapeDtyp...  35 us
    dot_general x1, matrix products, shards(): return jnp.dot(attended, weights, preferred_element_type=F32).astype(BF16)  2.16 us

profile of v11, /device:TPU:0, one launch (start us, length us, event | category | flops | bytes accessed | tf_op | source)
XLA Modules:
  0.0 37.2 jit_solution(1796089367439418464)
XLA Ops:
  0.0 35.0 %shard_map.91 = (bf16[256,1024]{1,0:T(8,128)(2,1)}, bf16[1024,256]{1,0:T(8,128)(2,1)}) custom-call(s32[16]{0:T(128)} %order_ref.1, s32[16,16]{1,0:T(8,128)} %adj_ref.1, f32[4]{0:T(128)} %temper_ref.1, f32[1,1024]{1,0:T(1,128)} %bitcast.3, bf16[256,256]{1,0:T(8,128)(2,1)} %tokens_ref.1, bf16[1024,256]{1,0:T(8,128)(2,1)} %wq_hbm.1, bf16[1024,256]{1,0:T(8,128)(2,1)} %wk_hbm.1, ...), custom_call_target="tpu_custom_call" | custom-call | tf_op jit(solution)/shard_map/pallas_call | solution.py:436
  35.0 2.2 %convolution_convert_fusion = bf16[256,256]{1,0:T(8,128)(2,1)} fusion(bf16[256,1024]{1,0:T(8,128)(2,1)} %get-tuple-element.7, bf16[1024,256]{1,0:T(8,128)(2,1)} %get-tuple-element.8), kind=kOutput, calls=%fused_computation | convolution fusion | flops 134283264 | bytes 1179648 | tf_op jit(solution)/shard_map/dot_general | solution.py:488
